TPU v7x, 256 devices: a whole 4x4x8 slice. The times are simulated.
256 devices in a mesh: pts: 16 (over x, y), tm: 16 (over z, core).
Axes of the slice: x: 4, y: 4, z: 8, core: 2. Of those that a mesh axis runs over, the one named last changes fastest.
Arguments:
- snapshots: bfloat16 [1024, 3, 131072], P('tm', None, 'pts'), may hold values from -13 to 13
- tail: bfloat16 [64, 3, 131072], P(None, None, 'pts'), may hold values from -13 to 13
- quad_weights: float32 [3, 131072], P(None, 'pts'), may hold values from 0.1 to 1
Outputs:
- modes: bfloat16 [64, 16, 2, 3, 131072], P('tm', None, None, None, 'pts')
All inputs are finite; a program needn't handle non-finite values.
Results may differ from a plain program's by a relative error of at most 0.0065.
Values may be sent and summed in bfloat16 or wider, within the bound.
No kernel may reach another device: no remote copies, remote signals or barrier semaphores. Data moves between devices by JAX's collectives and lax.ppermute only.
A program may use at most 64 MiB of HBM per device.

v0:
```python
import math

import jax
import jax.numpy as jnp
from jax import lax
from jax.sharding import PartitionSpec as P

NF = 64


def passed_along(value, axis, steps):
    count = lax.axis_size(axis)
    initial, last = (max(0, -steps), min(count, count - steps))
    return lax.ppermute(value, axis, [(source, source + steps) for source in range(initial, last)])


def window_table(length, freq_count):
    steps = jnp.arange(length, dtype=jnp.int32)
    freqs = jnp.arange(freq_count, dtype=jnp.int32)
    hann = 0.5 - 0.5 * jnp.cos(2.0 * math.pi * steps.astype(jnp.float32) / length)
    scale = 1.0 / jnp.sqrt(jnp.sum(hann * hann))
    phase = steps[:, None] * freqs[None, :] % length
    angle = 2.0 * math.pi * phase.astype(jnp.float32) / length
    real_part = (hann * scale)[:, None] * jnp.cos(angle)
    imag_part = -(hann * scale)[:, None] * jnp.sin(angle)
    return jnp.stack([real_part, imag_part], 2).reshape(length, 2 * freq_count).astype(jnp.bfloat16)


def product(pattern, left, right):
    return jnp.einsum(pattern, left, right, preferred_element_type=jnp.float32)


def spectra_of(halves, dft_table):
    block_count = halves.shape[0] - 1
    blocks = jnp.concatenate([halves[:-1], halves[1:]], 1)
    spectra = product("tk,btvp->bkvp", dft_table, blocks).astype(jnp.bfloat16)
    return spectra.reshape(
        block_count, dft_table.shape[1] // 2, 2, blocks.shape[2], blocks.shape[3]
    )


def gram_of(spectra, weights):
    weighted = (spectra.astype(jnp.float32) * weights).astype(jnp.bfloat16)
    spec_real, spec_imag = (spectra[:, :, 0], spectra[:, :, 1])
    wgt_real, wgt_imag = (weighted[:, :, 0], weighted[:, :, 1])
    pattern = "bfvp,cfvp->fbc"
    gram_real = product(pattern, wgt_real, spec_real) + product(pattern, wgt_imag, spec_imag)
    gram_imag = product(pattern, wgt_real, spec_imag) - product(pattern, wgt_imag, spec_real)
    return (gram_real, gram_imag)


def modes_of(spectra, gram_real, gram_imag, divisor):
    coef_real = (gram_real / divisor).astype(jnp.bfloat16)
    coef_imag = (gram_imag / divisor).astype(jnp.bfloat16)
    spec_real, spec_imag = (spectra[:, :, 0], spectra[:, :, 1])
    pattern = "bfvp,fbc->fcvp"
    mode_real = product(pattern, spec_real, coef_real) - product(pattern, spec_imag, coef_imag)
    mode_imag = product(pattern, spec_real, coef_imag) + product(pattern, spec_imag, coef_real)
    return jnp.stack([mode_real, mode_imag], 2).astype(jnp.bfloat16)


def shards(snapshots, tail, quad_weights):
    half_len, var_count, point_count = snapshots.shape
    dft_table = window_table(2 * half_len, NF)
    time_devices = lax.axis_size("tm")
    device_index = lax.axis_index("tm")
    divisor = var_count * point_count * lax.axis_size("pts")
    following = passed_along(snapshots, "tm", -1)
    following = jnp.where(device_index == time_devices - 1, tail, following)
    halves = jnp.stack([snapshots, following], 0)
    spectra = spectra_of(halves, dft_table)
    spectra = lax.all_to_all(spectra, "tm", split_axis=1, concat_axis=0, tiled=True)
    gram_real, gram_imag = gram_of(spectra, quad_weights)
    gram_real, gram_imag = lax.psum((gram_real, gram_imag), "pts")
    return modes_of(spectra, gram_real, gram_imag, divisor)


def solution(mesh):
    placed = (P("tm", None, "pts"), P(None, None, "pts"), P(None, "pts"))
    return jax.shard_map(
        shards,
        mesh=mesh,
        in_specs=placed,
        out_specs=P("tm", None, None, None, "pts"),
        check_vma=False,
    )
```

profile of v0, /device:TPU:64, one launch (start us, length us, event | category | flops | bytes accessed | tf_op | source)
XLA Modules:
  0.0 317.0 jit_solution(8275644265558282837)
XLA Ops:
  0.0 2.2 collective-permute-start
  2.2 0.6 multiply_reduce_fusion
  3.7 0.1 multiply_convert_fusion.3
  3.9 33.3 %collective-permute-done = bf16[64,3,8192]{2,0,1:T(8,128)(2,1)} collective-permute-done((bf16[64,3,8192]{2,0,1:T(8,128)(2,1)}, bf16[64,3,8192]{2,0,1:T(8,128)(2,1)}, u32[]{:S(2)}, u32[]{:S(2)}) %collective-permute-start) | collective-permute-done | bytes 3145760 | tf_op jit(solution)/shard_map/ppermute | solution.py:14
  37.3 2.2 select_bitcast_fusion
  39.5 3.7 %fusion = bf16[1,128,3,8192]{3,1,2,0:T(8,128)(2,1)} fusion(bf16[128,128,1]{0,1,2:T(8,128)(2,1)S(1)} %bitcast.100, bf16[1,64,3,8192]{3,1,2,0:T(8,128)(2,1)S(1)} %select_bitcast_fusion, bf16[1,64,3,8192]{3,1,2,0:T(8,128)(2,1)S(1)} %bitcast.99), kind=kOutput, calls=%fused_computation.2 | convolution fusion | flops 821035008 | bytes 12615680 | tf_op jit(solution)/shard_map/tk,btvp->bkvp/dot_general | solution.py:30
  43.2 10.8 %reshape.150 = bf16[1,64,2,3,8192]{4,2,1,3,0:T(2,128)(2,1)} reshape(bf16[1,128,3,8192]{3,1,2,0:T(8,128)(2,1)} %fusion) | data formatting | bytes 12582912 | tf_op jit(solution)/shard_map/reshape | solution.py:37
  54.1 5.9 %copy.37 = bf16[1,64,2,3,8192]{4,2,3,0,1:T(2,128)(2,1)S(1)} copy(bf16[1,64,2,3,8192]{4,2,1,3,0:T(2,128)(2,1)} %reshape.150) | data formatting | bytes 12582912 | tf_op jit(solution)/shard_map/reshape | solution.py:37
  60.0 147.8 %all_to_all.12 = bf16[1,64,2,3,8192]{4,2,3,0,1:T(2,128)(2,1)S(1)} all-to-all(bf16[1,64,2,3,8192]{4,2,3,0,1:T(2,128)(2,1)S(1)} %copy.37), channel_id=1, replica_groups=mesh['pts'=16,'tm'=16] {'tm'}, dimensions={1} | all-to-all | bytes 12582912 | tf_op jit(solution)/shard_map/all_to_all | solution.py:72
  207.8 4.3 %copy.38 = bf16[16,4,2,3,8192]{4,0,3,1,2:T(8,128)(2,1)S(1)} copy(bf16[16,4,2,3,8192]{4,2,3,1,0:T(2,128)(2,1)S(1)} %bitcast.97) | data formatting | bytes 12582912 | tf_op jit(solution)/shard_map/all_to_all | solution.py:72
  212.1 7.8 %multiply_convert_fusion = bf16[16,4,2,3,8192]{4,0,3,1,2:T(8,128)(2,1)} fusion(f32[3,8192]{1,0:T(4,128)S(1)} %copy-done.4, bf16[16,4,2,3,8192]{4,2,3,1,0:T(2,128)(2,1)S(1)} %bitcast.98), kind=kLoop, calls=%fused_computation | loop fusion | flops 9437184 | bytes 12681216 | tf_op jit(solution)/shard_map/convert_element_type | solution.py:43
  219.9 3.5 %fusion.14 = f32[4,16,16]{2,1,0:T(8,128)S(1)} fusion(bf16[16,4,2,3,8192]{4,0,3,1,2:T(8,128)(2,1)S(1)} %copy.38, bf16[16,4,2,3,8192]{4,0,3,1,2:T(8,128)(2,1)} %multiply_convert_fusion), kind=kOutput, calls=%fused_computation.25 | convolution fusion | flops 50331648 | bytes 6295552 | tf_op jit(solution)/shard_map/bfvp,cfvp->fbc/dot_general | solution.py:30
  223.3 0.3 copy-done.2
  223.6 1.4 fusion.13
  225.0 1.4 fusion.17
  226.5 1.2 fusion.18
  227.7 74.7 %all-reduce = (f32[4,16,16]{2,1,0:T(8,128)S(1)}, f32[4,16,16]{2,1,0:T(8,128)S(1)}) all-reduce(f32[4,16,16]{2,1,0:T(8,128)S(1)} %fusion.17, f32[4,16,16]{2,1,0:T(8,128)S(1)} %fusion.18), channel_id=1, replica_groups=mesh['pts'=16,'tm'=16] {'pts'}, use_global_device_ids=true, to_apply=%region_2.3 | all-reduce | flops 2048 | bytes 16384 | tf_op jit(solution)/shard_map/psum | solution.py:74
  302.5 3.1 fusion.11
  305.5 0.7 copy-done.1
  306.2 1.0 fusion.12
  307.2 1.3 fusion.3
  308.5 1.3 fusion.4
  309.8 0.6 pad_maximum_fusion
  310.4 6.7 %copy.45 = bf16[4,16,2,3,8192]{4,2,3,1,0:T(2,128)(2,1)} copy(bf16[4,16,2,3,8192]{4,1,3,0,2:T(8,128)(2,1)S(1)} %pad_maximum_fusion) | data formatting | bytes 12582912 | tf_op jit(solution)/shard_map/stack | solution.py:59
  (12 shorter events, 0.2 us)
Async XLA Ops:
  0.0 39.5 %copy-start.3 = (bf16[64,3,8192]{2,0,1:T(8,128)(2,1)S(1)}, bf16[64,3,8192]{2,0,1:T(8,128)(2,1)}, u32[]{:S(2)}) copy-start(bf16[64,3,8192]{2,0,1:T(8,128)(2,1)} %param.3) | copy-start | bytes 9437188
  0.0 37.3 %collective-permute-start = (bf16[64,3,8192]{2,0,1:T(8,128)(2,1)}, bf16[64,3,8192]{2,0,1:T(8,128)(2,1)}, u32[]{:S(2)}, u32[]{:S(2)}) collective-permute-start(bf16[64,3,8192]{2,0,1:T(8,128)(2,1)} %param.3), channel_id=1, source_target_pairs={{1,0},{2,1},{3,2},{4,3},{5,4},{6,5},{7,6},{8,7},{9,8},{10,9},{11,1... | collective-permute-start | bytes 9437192 | tf_op jit(solution)/shard_map/ppermute | solution.py:14
  207.8 4.3 %copy-start.4 = (f32[3,8192]{1,0:T(4,128)S(1)}, f32[3,8192]{1,0:T(4,128)}, u32[]{:S(2)}) copy-start(f32[3,8192]{1,0:T(4,128)} %param.5) | copy-start | bytes 294916
  212.1 14.4 %copy-start = (bf16[16,4,2,3,8192]{4,0,3,1,2:T(8,128)(2,1)}, bf16[16,4,2,3,8192]{4,0,3,1,2:T(8,128)(2,1)S(1)}, u32[]{:S(2)}) copy-start(bf16[16,4,2,3,8192]{4,0,3,1,2:T(8,128)(2,1)S(1)} %copy.38) | copy-start | bytes 18874372
  219.9 3.7 %copy-start.2 = (bf16[16,4,2,3,8192]{4,0,3,1,2:T(8,128)(2,1)S(1)}, bf16[16,4,2,3,8192]{4,0,3,1,2:T(8,128)(2,1)}, u32[]{:S(2)}) copy-start(bf16[16,4,2,3,8192]{4,0,3,1,2:T(8,128)(2,1)} %multiply_convert_fusion) | copy-start | bytes 18874372
  302.5 3.7 %copy-start.1 = (bf16[16,4,2,3,8192]{4,0,3,1,2:T(8,128)(2,1)S(1)}, bf16[16,4,2,3,8192]{4,0,3,1,2:T(8,128)(2,1)}, u32[]{:S(2)}) copy-start(bf16[16,4,2,3,8192]{4,0,3,1,2:T(8,128)(2,1)} %copy-done) | copy-start | bytes 18874372
where the time goes:
time: 317 us
  blocking collectives  223 us (70%)
  waiting for transfers between devices  33.3 us (11%)
  local copies, waits for them, and re-layouts  28.7 us (9%)
  matrix products  17.9 us (6%)
  other arithmetic  11.6 us (4%)
    all_to_all x1, blocking collectives, shards(): lax.all_to_all(spectra, 'tm', split_axis=1, concat_axis=0, tiled=True)  148 us
    psum x1, blocking collectives, shards(): gram_real, gram_imag = lax.psum((gram_real, gram_imag), 'pts')  74.7 us
    ppermute x1, waiting for transfers between devices, passed_along(): lax.ppermute(value, axis, [(source, source + steps) for source in range(i...  33.3 us
    dot_general x9, matrix products, product(): return jnp.einsum(pattern, left, right, preferred_element_type=jnp.float32)  17.9 us
    reshape x2, local copies, waits for them, and re-layouts, spectra_of(): spectra.reshape(block_count, dft_table.shape[1] // 2, 2, blocks.shape[2],...  16.8 us
    convert_element_type x1, other arithmetic, gram_of(): weighted = (spectra.astype(jnp.float32) * weights).astype(jnp.bfloat16)  7.78 us
    another operation x1, local copies, waits for them, and re-layouts, modes_of(): return jnp.stack([mode_real, mode_imag], 2).astype(jnp.bfloat16)  6.69 us
  transfers between devices with their start and end apart: 1, of which 1 were waited for; matrix products, arithmetic and copies ran while one was open for 0% of the time, Pallas kernels for 0%

commit v1 on v0

v1 whole, which is shorter than its diff:
```python
import math

import jax
import jax.numpy as jnp
import numpy as np
from jax import lax
from jax.experimental import pallas as pl
from jax.experimental.pallas import tpu as pltpu
from jax.sharding import PartitionSpec as P

NF = 64
NFFT = 128
HALF = 64
VARS = 3
NB = 16
OWN = 4
CHIPS = 8
ROWS = 128
CHUNK = 1024
VMEM_LIMIT = 40 * 1024 * 1024


def window_table():
    steps = np.arange(NFFT)
    freqs = np.arange(NF)
    hann = 0.5 - 0.5 * np.cos(2.0 * math.pi * steps / NFFT)
    scale = 1.0 / np.sqrt(np.sum(hann * hann))
    angle = 2.0 * math.pi * (steps[:, None] * freqs[None, :] % NFFT) / NFFT
    real_part = (hann * scale)[:, None] * np.cos(angle)
    imag_part = -(hann * scale)[:, None] * np.sin(angle)
    table = np.stack([real_part, imag_part], 2).reshape(NFFT, 2 * NF).T
    return np.stack([table, np.roll(table, HALF, axis=1)]).astype(jnp.bfloat16)


def row_facts():
    row = np.arange(ROWS)
    chip, odd, freq, part = row // 16, row // 8 % 2, row // 2 % 4, row % 2
    block = np.stack([2 * chip + odd, (2 * chip - odd) % NB])
    return block, freq, part


def gram_selectors():
    block, freq, part = row_facts()
    same = freq[:, None] == freq[None, :]
    real = (same & (part[:, None] == part[None, :])).astype(np.float32)
    sign = np.where(part[:, None] == 0, 1.0, -1.0)
    imag = (same & (part[:, None] != part[None, :])) * sign
    masks = np.stack([real, imag]).astype(np.float32)
    left = (np.arange(NB)[None, :, None] == block[:, None, :]).astype(np.float32)
    col = np.arange(ROWS)
    col_part, col_freq, col_block = col // 64, col // 16 % 4, col % 16
    hit = (block[:, :, None] == col_block) & (freq[None, :, None] == col_freq)
    right = np.stack([hit & (col_part == 0), hit & (col_part == 1)], 1).astype(np.float32)
    return masks, left, right


def mode_selectors():
    block, freq, part = row_facts()
    left = (block[:, :, None] == np.arange(NB)).astype(jnp.bfloat16)
    col = np.arange(ROWS)
    col_part, col_freq, col_block = col // 64, col // 16 % 4, col % 16
    out_freq, out_block, out_part = col // 32, col // 2 % 16, col % 2
    hit = (col_freq[:, None] == out_freq) & (col_block[:, None] == out_block)
    right = np.stack([hit & (col_part[:, None] == 0), hit & (col_part[:, None] == 1)]).astype(jnp.bfloat16)
    same = freq[:, None] == out_freq[None, :]
    real = (same & (part[:, None] == out_part[None, :])).astype(np.float32)
    sign = np.where(out_part[None, :] == 0, -1.0, 1.0)
    imag = (same & (part[:, None] != out_part[None, :])) * sign
    return left, right, np.stack([real, imag]).astype(np.float32)


def dft_kernel(flags, table, own, beside, halo, tail, out):
    tbl = table[0]
    first = jnp.where(flags[1] == 1, tail[0], beside[0])
    second = jnp.where(flags[2] == 1, tail[0], halo[0])
    even = jnp.concatenate([own[0], beside[0]], 0)
    odd = jnp.concatenate([first, second], 0)
    even = jnp.dot(tbl, even, preferred_element_type=jnp.float32)
    odd = jnp.dot(tbl, odd, preferred_element_type=jnp.float32)
    width = even.shape[1]
    both = jnp.concatenate([even.reshape(16, 8, width), odd.reshape(16, 8, width)], 1)
    out[:, 0] = both.astype(jnp.bfloat16)


def dft_call(flags, record, beside, halo, tail):
    table = jnp.asarray(window_table())
    points = record.shape[2]
    part = points // 2
    count = part // CHUNK
    piece = pl.BlockSpec((1, HALF, CHUNK), lambda v, i, flags: (v, 0, i))
    mine = pl.BlockSpec((1, HALF, CHUNK), lambda v, i, flags: (v, 0, flags[0] * count + i))
    return pl.pallas_call(
        dft_kernel,
        grid_spec=pltpu.PrefetchScalarGridSpec(
            num_scalar_prefetch=1,
            grid=(VARS, count),
            in_specs=[
                pl.BlockSpec((1, ROWS, NFFT), lambda v, i, flags: (flags[0], 0, 0)),
                mine,
                piece,
                piece,
                mine,
            ],
            out_specs=pl.BlockSpec((16, 1, 16, CHUNK), lambda v, i, flags: (0, v, 0, i)),
        ),
        out_shape=jax.ShapeDtypeStruct((16, VARS, 16, part), jnp.bfloat16),
        compiler_params=pltpu.CompilerParams(vmem_limit_bytes=VMEM_LIMIT),
        name="dft",
    )(flags, table, record, beside, halo, tail)


def exact_dot(left, right):
    return jnp.dot(left, right, precision=lax.Precision.HIGHEST, preferred_element_type=jnp.float32)


def gram_kernel(spectra, weights, masks, left, right, out, total):
    half, step = pl.program_id(0), pl.program_id(1)

    @pl.when(step == 0)
    def _():
        total[half] = jnp.zeros((ROWS, ROWS), jnp.float32)

    acc = total[half]
    for v in range(VARS):
        spec = spectra[:, 0, v].reshape(ROWS, CHUNK)
        wgt = weights[v : v + 1, :]
        weighted = (spec.astype(jnp.float32) * wgt).astype(jnp.bfloat16)
        acc = acc + lax.dot_general(
            weighted, spec, (((1,), (1,)), ((), ())), preferred_element_type=jnp.float32
        )
    total[half] = acc

    @pl.when((half == 1) & (step == pl.num_programs(1) - 1))
    def _():
        gram = jnp.zeros((NB, ROWS), jnp.float32)
        for k in range(2):
            for part in range(2):
                picked = exact_dot(left[k], total[k] * masks[part])
                gram = gram + exact_dot(picked, right[k, part])
        out[...] = jnp.broadcast_to(gram[None], out.shape)


def gram_call(spectra, weights, copies):
    masks, left, right = gram_selectors()
    part = spectra.shape[-1]
    count = part // CHUNK
    whole = lambda shape: pl.BlockSpec(shape, lambda k, i: (0,) * len(shape))
    return pl.pallas_call(
        gram_kernel,
        grid=(2, count),
        in_specs=[
            pl.BlockSpec((CHIPS, 1, VARS, 16, CHUNK), lambda k, i: (0, k, 0, 0, i)),
            pl.BlockSpec((VARS, CHUNK), lambda k, i: (0, k * count + i)),
            whole(masks.shape),
            whole(left.shape),
            whole(right.shape),
        ],
        out_specs=whole((copies, NB, ROWS)),
        out_shape=jax.ShapeDtypeStruct((copies, NB, ROWS), jnp.float32),
        scratch_shapes=[pltpu.VMEM((2, ROWS, ROWS), jnp.float32)],
        compiler_params=pltpu.CompilerParams(vmem_limit_bytes=VMEM_LIMIT),
        name="gram",
    )(spectra, weights, jnp.asarray(masks), jnp.asarray(left), jnp.asarray(right))


def modes_kernel(divisor, grams, left, right, masks, spectra, out, matrix):
    half, step = pl.program_id(0), pl.program_id(1)

    @pl.when((half == 0) & (step == 0))
    def _():
        coef = (jnp.sum(grams[...], 0) / divisor).astype(jnp.bfloat16)
        for k in range(2):
            rows = jnp.dot(left[k], coef, preferred_element_type=jnp.float32).astype(jnp.bfloat16)
            real = jnp.dot(rows, right[0], preferred_element_type=jnp.float32)
            imag = jnp.dot(rows, right[1], preferred_element_type=jnp.float32)
            full = real * masks[0] + imag * masks[1]
            matrix[k] = full.T.astype(jnp.bfloat16)

    mat = matrix[half]
    for v in range(VARS):
        spec = spectra[:, 0, v].reshape(ROWS, CHUNK)
        modes = jnp.dot(mat, spec, preferred_element_type=jnp.float32).astype(jnp.bfloat16)
        out[:, :, v] = modes.reshape(OWN, NB, 2, CHUNK)


def modes_call(grams, spectra, divisor):
    left, right, masks = mode_selectors()
    part = spectra.shape[-1]
    count = part // CHUNK
    whole = lambda shape: pl.BlockSpec(shape, lambda k, i: (0,) * len(shape))
    return pl.pallas_call(
        lambda *refs: modes_kernel(divisor, *refs),
        grid=(2, count),
        in_specs=[
            whole(grams.shape),
            whole(left.shape),
            whole(right.shape),
            whole(masks.shape),
            pl.BlockSpec((CHIPS, 1, VARS, 16, CHUNK), lambda k, i: (0, k, 0, 0, i)),
        ],
        out_specs=pl.BlockSpec((OWN, NB, VARS, 2, CHUNK), lambda k, i: (0, 0, 0, 0, k * count + i)),
        out_shape=jax.ShapeDtypeStruct((OWN, NB, VARS, 2, 2 * part), jnp.bfloat16),
        scratch_shapes=[pltpu.VMEM((2, ROWS, ROWS), jnp.bfloat16)],
        compiler_params=pltpu.CompilerParams(vmem_limit_bytes=VMEM_LIMIT),
        name="modes",
    )(grams, jnp.asarray(left), jnp.asarray(right), jnp.asarray(masks), spectra)


def shards(snapshots, tail, quad_weights):
    points = snapshots.shape[2]
    part = points // 2
    index = lax.axis_index("tm")
    core, chip = index % 2, index // 2
    record = jnp.transpose(snapshots, (1, 0, 2))
    tail = jnp.transpose(tail, (1, 0, 2))
    own = lax.dynamic_slice_in_dim(record, core * part, part, 2)
    other = lax.dynamic_slice_in_dim(record, (1 - core) * part, part, 2)
    before = [(2 * z + 2, 2 * z) for z in range(CHIPS - 1)]
    after = [((2 * z - 1) % NB, 2 * z + 1) for z in range(CHIPS)]
    halo = lax.ppermute(own, "tm", before + after)
    beside = lax.ppermute(other, "tm", [(i, i ^ 1) for i in range(NB)])
    flags = jnp.stack([core, (index == 1).astype(jnp.int32), (index == NB - 2).astype(jnp.int32)])
    spectra = dft_call(flags, record, beside, halo, tail)
    spectra = lax.all_to_all(spectra, "tm", split_axis=0, concat_axis=0, tiled=True)
    spectra = spectra.reshape(CHIPS, 2, VARS, 16, part)
    slabs = lax.axis_size("pts")
    grams = gram_call(spectra, quad_weights, slabs)
    grams = lax.all_to_all(grams, "pts", split_axis=0, concat_axis=0, tiled=True)
    modes = modes_call(grams, spectra, float(VARS * points * slabs))
    return jnp.transpose(modes, (0, 1, 3, 2, 4))


def solution(mesh):
    placed = (P("tm", None, "pts"), P(None, None, "pts"), P(None, "pts"))
    return jax.shard_map(
        shards,
        mesh=mesh,
        in_specs=placed,
        out_specs=P("tm", None, None, None, "pts"),
        check_vma=False,
    )
```

time: 317 us -> 215 us (0.68)
  the two profiles are of different devices: /device:TPU:64 before, /device:TPU:1 now
where the time goes in v1:
time: 215 us
  blocking collectives  161 us (75%)
  waiting for transfers between devices  21.7 us (10%)
  Pallas kernels  21.4 us (10%)
  local copies, waits for them, and re-layouts  6 us (3%)
  starting transfers between devices  4.61 us (2%)
    all_to_all x1, blocking collectives, shards(): lax.all_to_all(spectra, 'tm', split_axis=0, concat_axis=0, tiled=True)  147 us
    ppermute x1, waiting for transfers between devices, shards(): halo = lax.ppermute(own, 'tm', before + after)  21.7 us
    all_to_all x1, blocking collectives, shards(): lax.all_to_all(grams, 'pts', split_axis=0, concat_axis=0, tiled=True)  13.6 us
    pallas_call x1, Pallas kernels, dft_call(): pl.pallas_call(dft_kernel, grid_spec=pltpu.PrefetchScalarGridSpec(num_sca...  10.7 us
    pallas_call x1, Pallas kernels, modes_call(): pl.pallas_call(lambda *refs: modes_kernel(divisor, *refs), grid=(2, count...  6.23 us
    pallas_call x1, Pallas kernels, gram_call(): pl.pallas_call(gram_kernel, grid=(2, count), in_specs=[pl.BlockSpec((CHIP...  4.52 us
    ppermute x1, starting transfers between devices, shards(): halo = lax.ppermute(own, 'tm', before + after)  4.36 us
  transfers between devices with their start and end apart: 2, of which 1 were waited for; matrix products, arithmetic and copies ran while one was open for 0% of the time, Pallas kernels for 0%

profile of v1, /device:TPU:1, one launch (start us, length us, event | category | flops | bytes accessed | tf_op | source)
XLA Modules:
  0.0 214.7 jit_solution(9732628530342722803)
XLA Ops:
  0.0 4.1 %dynamic-slice_bitcast_fusion = (bf16[3,64,4096]{2,1,0:T(8,128)(2,1)}, bf16[3,64,4096]{2,1,0:T(8,128)(2,1)}) fusion(bf16[64,3,8192]{2,0,1:T(8,128)(2,1)} %param.10, s32[]{:T(128)S(6)} %select_n.15, s32[]{:T(128)S(6)} %select_n.14), kind=kLoop, calls=%fused_computation | loop fusion | bytes 6291464 | tf_op jit(solution)/shard_map/dynamic_slice | solution.py:216
  4.1 4.4 %collective-permute-start.1 = (bf16[3,64,4096]{2,1,0:T(8,128)(2,1)}, bf16[3,64,4096]{2,1,0:T(8,128)(2,1)}, u32[]{:S(2)}, u32[]{:S(2)}) collective-permute-start(bf16[3,64,4096]{2,1,0:T(8,128)(2,1)} %get-tuple-element.5), channel_id=1, source_target_pairs={{2,0},{4,2},{6,4},{8,6},{10,8},{12,10},{14,12},{15,1},{1,3},{3,5},... | collective-permute-start | bytes 4718600 | tf_op jit(solution)/shard_map/ppermute | solution.py:220
  8.4 0.2 collective-permute-start
  8.7 0.1 pad_add_fusion.flags
  8.8 21.7 %collective-permute-done.1.halo = bf16[3,64,4096]{2,1,0:T(8,128)(2,1)} collective-permute-done((bf16[3,64,4096]{2,1,0:T(8,128)(2,1)}, bf16[3,64,4096]{2,1,0:T(8,128)(2,1)}, u32[]{:S(2)}, u32[]{:S(2)}) %collective-permute-start.1) | collective-permute-done | bytes 1572896 | tf_op jit(solution)/shard_map/ppermute | solution.py:220
  30.5 0.0 collective-permute-done.beside
  30.5 0.0 copy-done
  30.5 0.0 copy-done.8
  30.5 0.0 copy-start.1
  30.5 1.9 copy-done.1
  32.4 10.7 %dft.1 = bf16[16,3,16,4096]{3,2,1,0:T(8,128)(2,1)} custom-call(s32[3]{0:T(128)S(1)} %pad_add_fusion.flags, bf16[2,128,128]{2,1,0:T(8,128)(2,1)S(1)} %copy-done.8, bf16[3,64,8192]{2,1,0:T(8,128)(2,1)S(1)} %bitcast.13, bf16[3,64,4096]{2,1,0:T(8,128)(2,1)} %collective-permute-done.beside, bf16[3,64,4096]{2,1,0:T(8,128)(2,1)} %collective-permute-done.1.halo, ...), custom_call_target="tpu_custom_call" | custom-call | tf_op jit(solution)/shard_map/dft/pallas_call | solution.py:92
  43.1 0.0 copy-start.9
  43.1 147.2 %all_to_all.10 = bf16[16,3,16,4096]{3,2,1,0:T(8,128)(2,1)S(1)} all-to-all(bf16[16,3,16,4096]{3,2,1,0:T(8,128)(2,1)} %dft.1), channel_id=1, replica_groups=mesh['pts'=16,'tm'=16] {'tm'}, dimensions={0} | all-to-all | bytes 12582912 | tf_op jit(solution)/shard_map/all_to_all | solution.py:224
  190.3 0.0 copy-done.2
  190.3 0.0 copy-done.4
  190.3 0.0 copy-done.5
  190.3 0.0 copy-done.9
  190.3 0.0 copy-start.3
  190.3 0.0 copy-start.6
  190.3 0.0 copy-start.7
  190.4 4.5 %gram.1 = f32[16,16,128]{2,1,0:T(8,128)S(1)} custom-call(bf16[8,2,3,16,4096]{4,3,2,1,0:T(8,128)(2,1)S(1)} %bitcast.11, f32[3,8192]{1,0:T(4,128)S(1)} %copy-done.4, f32[2,128,128]{2,1,0:T(8,128)S(1)} %copy-done.5, f32[2,16,128]{2,1,0:T(8,128)S(1)} %copy-done.9, f32[2,2,128,128]{3,2,1,0:T(8,128)S(1)} %copy-done.2), custom_call_target="tpu_custom_call" | custom-call | tf_op jit(solution)/shard_map/gram/pallas_call | solution.py:148
  194.9 13.6 %all_to_all.11.refs_0_ = f32[16,16,128]{2,1,0:T(8,128)S(1)} all-to-all(f32[16,16,128]{2,1,0:T(8,128)S(1)} %gram.1), channel_id=1, replica_groups=mesh['pts'=16,'tm'=16] {'pts'}, dimensions={0} | all-to-all | bytes 262144 | tf_op jit(solution)/shard_map/all_to_all | solution.py:228
  208.4 0.0 copy-done.6
  208.4 6.2 %modes.1 = bf16[4,16,3,2,8192]{4,3,2,1,0:T(2,128)(2,1)} custom-call(f32[16,16,128]{2,1,0:T(8,128)S(1)} %all_to_all.11.refs_0_, bf16[2,128,16]{2,1,0:T(8,128)(2,1)S(1)} %copy-done.7, bf16[2,128,128]{2,1,0:T(8,128)(2,1)S(1)} %copy-done.6, f32[2,128,128]{2,1,0:T(8,128)S(1)} %copy-done.3, bf16[8,2,3,16,4096]{4,3,2,1,0:T(8,128)(2,1)S(1)} %bitcast.12), custom_call_target="tpu_custom_call" | custom-call | tf_op jit(solution)/shard_map/modes/pallas_call | solution.py:191
  (7 shorter events, 0.0 us)
Async XLA Ops:
  0.0 30.5 %copy-start = (bf16[64,3,8192]{2,0,1:T(8,128)(2,1)S(1)}, bf16[64,3,8192]{2,0,1:T(8,128)(2,1)}, u32[]{:S(2)}) copy-start(bf16[64,3,8192]{2,0,1:T(8,128)(2,1)} %param.10) | copy-start | bytes 9437188
  0.0 30.5 %copy-start.8 = (bf16[2,128,128]{2,1,0:T(8,128)(2,1)S(1)}, bf16[2,128,128]{2,1,0:T(8,128)(2,1)}, u32[]{:S(2)}) copy-start(bf16[2,128,128]{2,1,0:T(8,128)(2,1)} %constant.39.clone.table) | copy-start | bytes 196612
  4.1 26.4 %collective-permute-start.1 = (bf16[3,64,4096]{2,1,0:T(8,128)(2,1)}, bf16[3,64,4096]{2,1,0:T(8,128)(2,1)}, u32[]{:S(2)}, u32[]{:S(2)}) collective-permute-start(bf16[3,64,4096]{2,1,0:T(8,128)(2,1)} %get-tuple-element.5), channel_id=1, source_target_pairs={{2,0},{4,2},{6,4},{8,6},{10,8},{12,10},{14,12},{15,1},{1,3},{3,5},... | collective-permute-start | bytes 4718600 | tf_op jit(solution)/shard_map/ppermute | solution.py:220
  8.4 22.0 %collective-permute-start = (bf16[3,64,4096]{2,1,0:T(8,128)(2,1)}, bf16[3,64,4096]{2,1,0:T(8,128)(2,1)}, u32[]{:S(2)}, u32[]{:S(2)}) collective-permute-start(bf16[3,64,4096]{2,1,0:T(8,128)(2,1)} %get-tuple-element.6), channel_id=1, source_target_pairs={{0,1},{1,0},{2,3},{3,2},{4,5},{5,4},{6,7},{7,6},{8,9},{9,8},{10,11... | collective-permute-start | bytes 4718600 | tf_op jit(solution)/shard_map/ppermute | solution.py:221
  30.5 1.9 copy-start.1
  43.0 147.2 %copy-start.2 = (f32[2,2,128,128]{3,2,1,0:T(8,128)S(1)}, f32[2,2,128,128]{3,2,1,0:T(8,128)}, u32[]{:S(2)}) copy-start(f32[2,2,128,128]{3,2,1,0:T(8,128)} %constant.42.clone.right) | copy-start | bytes 786436
  43.1 147.3 %copy-start.4 = (f32[3,8192]{1,0:T(4,128)S(1)}, f32[3,8192]{1,0:T(4,128)}, u32[]{:S(2)}) copy-start(f32[3,8192]{1,0:T(4,128)} %weights.1) | copy-start | bytes 294916
  43.1 147.3 %copy-start.5 = (f32[2,128,128]{2,1,0:T(8,128)S(1)}, f32[2,128,128]{2,1,0:T(8,128)}, u32[]{:S(2)}) copy-start(f32[2,128,128]{2,1,0:T(8,128)} %constant.40.clone.masks) | copy-start | bytes 393220
  43.1 147.3 %copy-start.9 = (f32[2,16,128]{2,1,0:T(8,128)S(1)}, f32[2,16,128]{2,1,0:T(8,128)}, u32[]{:S(2)}) copy-start(f32[2,16,128]{2,1,0:T(8,128)} %constant.41.clone.left) | copy-start | bytes 49156
  190.3 18.1 %copy-start.3 = (f32[2,128,128]{2,1,0:T(8,128)S(1)}, f32[2,128,128]{2,1,0:T(8,128)}, u32[]{:S(2)}) copy-start(f32[2,128,128]{2,1,0:T(8,128)} %constant.45.clone.refs_3_) | copy-start | bytes 393220
  190.3 18.1 %copy-start.6 = (bf16[2,128,128]{2,1,0:T(8,128)(2,1)S(1)}, bf16[2,128,128]{2,1,0:T(8,128)(2,1)}, u32[]{:S(2)}) copy-start(bf16[2,128,128]{2,1,0:T(8,128)(2,1)} %constant.44.clone.refs_2_) | copy-start | bytes 196612
  190.3 18.1 %copy-start.7 = (bf16[2,128,16]{2,1,0:T(8,128)(2,1)S(1)}, bf16[2,128,16]{2,1,0:T(8,128)(2,1)}, u32[]{:S(2)}) copy-start(bf16[2,128,16]{2,1,0:T(8,128)(2,1)} %constant.43.clone.refs_1_) | copy-start | bytes 24580

commit v2 on v0

v2 whole, which is shorter than its diff:
```python
import math

import jax
import jax.numpy as jnp
import numpy as np
from jax import lax
from jax.experimental import pallas as pl
from jax.experimental.pallas import tpu as pltpu
from jax.sharding import PartitionSpec as P

NF = 64
NFFT = 128
HALF = 64
VARS = 3
NB = 16
OWN = 4
CHIPS = 8
ROWS = 128
CHUNK = 1024
WIDE = 4096
VMEM_LIMIT = 28 * 1024 * 1024
SHIFTS = (4, 3, 5, 2, 6, 1, 7, 0)


def window_tables():
    steps = np.arange(NFFT)
    freqs = np.arange(NF)
    hann = 0.5 - 0.5 * np.cos(2.0 * math.pi * steps / NFFT)
    scale = 1.0 / np.sqrt(np.sum(hann * hann))
    angle = 2.0 * math.pi * (steps[:, None] * freqs[None, :] % NFFT) / NFFT
    real_part = (hann * scale)[:, None] * np.cos(angle)
    imag_part = -(hann * scale)[:, None] * np.sin(angle)
    table = np.stack([real_part, imag_part], 2).reshape(NFFT, 2 * NF).T.astype(jnp.bfloat16)
    rows = table.reshape(CHIPS, 2, 2 * OWN, NFFT).transpose(1, 0, 2, 3)
    shifted = np.stack([rows[i % 2][[(i // 2 + shift) % CHIPS for shift in SHIFTS]] for i in range(NB)])
    swapped = np.stack([rows[0], np.roll(rows[1], HALF, axis=-1)])
    return swapped.reshape(2, ROWS // 2, NFFT), shifted.reshape(NB, ROWS // 2, NFFT)


def iota(shape, axis):
    return lax.broadcasted_iota(jnp.int32, shape, axis)


def row_facts(shape, axis, chip):
    row = iota(shape, axis)
    odd, place = row >> 7, (row >> 4) & 7
    half, freq, part = (row >> 3) & 1, (row >> 1) & 3, row & 1
    shift = sum(jnp.where(place == at, shift, 0) for at, shift in enumerate(SHIFTS))
    source = jnp.where(odd == 1, (chip - shift) & 7, place)
    block = (2 * source + jnp.where(odd == 1, 1 - 2 * half, 0)) & (NB - 1)
    return block, freq, part, half


def dft_even_kernel(flags, table, own_a, own_b, beside_a, beside_b, out):
    def spectrum(first, second):
        both = jnp.concatenate([first[0], second[0]], 0)
        freqs = jnp.dot(table[0], both, preferred_element_type=jnp.float32)
        return freqs.reshape(CHIPS, 2 * OWN, freqs.shape[1])

    both = jnp.concatenate([spectrum(own_a, beside_a), spectrum(own_b, beside_b)], 1)
    out[:, 0] = both.astype(jnp.bfloat16)


def dft_even(flags, record, beside):
    table, _ = window_tables()
    part = record.shape[2] // 2
    count = part // WIDE
    low = pl.BlockSpec((1, HALF, WIDE), lambda v, i, flags: (v, 0, i))
    high = pl.BlockSpec((1, HALF, WIDE), lambda v, i, flags: (v, 0, count + i))
    return pl.pallas_call(
        dft_even_kernel,
        grid_spec=pltpu.PrefetchScalarGridSpec(
            num_scalar_prefetch=1,
            grid=(VARS, count),
            in_specs=[
                pl.BlockSpec((1, ROWS // 2, NFFT), lambda v, i, flags: (flags[0] & 1, 0, 0)),
                low,
                high,
                low,
                high,
            ],
            out_specs=pl.BlockSpec((CHIPS, 1, 16, WIDE), lambda v, i, flags: (0, v, 0, i)),
        ),
        out_shape=jax.ShapeDtypeStruct((CHIPS, VARS, 16, part), jnp.bfloat16),
        compiler_params=pltpu.CompilerParams(vmem_limit_bytes=VMEM_LIMIT),
        name="dft_even",
    )(flags, jnp.asarray(table), record, record, beside, beside)


def dft_odd_kernel(flags, table, own_a, own_b, beside_a, beside_b, halo, swapped, tail_a, tail_b, *outs):
    core, chip = flags[0] & 1, flags[0] >> 1
    pick = lambda cond, yes, no: jnp.where(cond, yes[0], no[0])
    first_a = pick(core == 1, own_a, beside_a)
    second_a = jnp.where(chip == CHIPS - 1, tail_a[0], pick(core == 1, swapped, halo))
    first_b = pick(core == 1, halo, swapped)
    second_b = jnp.where(chip == 0, tail_b[0], pick(core == 1, beside_b, own_b))

    def spectrum(first, second):
        both = jnp.concatenate([first, second], 0)
        freqs = jnp.dot(table[0], both, preferred_element_type=jnp.float32)
        return freqs.reshape(CHIPS, 2 * OWN, freqs.shape[1])

    both = jnp.concatenate([spectrum(first_a, second_a), spectrum(first_b, second_b)], 1)
    both = both.astype(jnp.bfloat16)
    for place, out in enumerate(outs):
        out[0] = both[place]


def dft_odd(flags, record, beside, halo, swapped, tail):
    _, table = window_tables()
    part = record.shape[2] // 2
    count = part // WIDE
    table_spec = pl.BlockSpec((1, ROWS // 2, NFFT), lambda v, i, flags: (flags[0], 0, 0))
    low = pl.BlockSpec((1, HALF, WIDE), lambda v, i, flags: (v, 0, i))
    high = pl.BlockSpec((1, HALF, WIDE), lambda v, i, flags: (v, 0, count + i))
    low_out = pl.BlockSpec((1, 16, WIDE), lambda v, i, flags: (v, 0, i))
    return pl.pallas_call(
        dft_odd_kernel,
        grid_spec=pltpu.PrefetchScalarGridSpec(
            num_scalar_prefetch=1,
            grid=(VARS, count),
            in_specs=[table_spec, low, high, low, high, low, low, low, high],
            out_specs=[low_out] * CHIPS,
        ),
        out_shape=[jax.ShapeDtypeStruct((VARS, 16, part), jnp.bfloat16)] * CHIPS,
        compiler_params=pltpu.CompilerParams(vmem_limit_bytes=VMEM_LIMIT),
        name="dft_odd",
    )(flags, jnp.asarray(table), record, record, beside, beside, halo, swapped, tail, tail)


def exact_dot(left, right):
    return jnp.dot(left, right, precision=lax.Precision.HIGHEST, preferred_element_type=jnp.float32)


def rows_of(pieces, v):
    evens = pieces[0][:, v].reshape(ROWS, pieces[0].shape[-1])
    return jnp.concatenate([evens, *(piece[v] for piece in pieces[1:])], 0)


def gram_kernel(flags, weights_a, weights_b, *refs):
    pieces, out, total = refs[:-2], refs[-2], refs[-1]
    step = pl.program_id(0)

    @pl.when(step == 0)
    def _():
        total[...] = jnp.zeros(total.shape, jnp.float32)

    size = 2 * ROWS
    acc = total[...]
    for v in range(VARS):
        spec = rows_of(pieces, v)
        wgt_a, wgt_b = weights_a[v : v + 1, :], weights_b[v : v + 1, :]
        wgt = jnp.concatenate([jnp.broadcast_to(wgt_a, (8, CHUNK)), jnp.broadcast_to(wgt_b, (8, CHUNK))], 0)
        wide = spec.astype(jnp.float32).reshape(16, 16, CHUNK) * wgt[None]
        weighted = wide.reshape(size, CHUNK).astype(jnp.bfloat16)
        acc = acc + lax.dot_general(
            weighted, spec, (((1,), (1,)), ((), ())), preferred_element_type=jnp.float32
        )
    total[...] = acc

    @pl.when(step == pl.num_programs(0) - 1)
    def _():
        chip = flags[0] >> 1
        _, freq_i, part_i, half_i = row_facts((size, size), 0, chip)
        _, freq_j, part_j, half_j = row_facts((size, size), 1, chip)
        same = (freq_i == freq_j) & (half_i == half_j)
        sums = total[...]
        real = jnp.where(same & (part_i == part_j), sums, 0.0)
        imag = jnp.where(same & (part_i != part_j), jnp.where(part_i == 0, sums, -sums), 0.0)
        block, _, _, _ = row_facts((NB, size), 1, chip)
        left = (iota((NB, size), 0) == block).astype(jnp.float32)
        block, freq, _, _ = row_facts((size, ROWS), 0, chip)
        col = iota((size, ROWS), 1)
        hit = (block == (col & 15)) & (freq == ((col >> 4) & 3))
        right_real = (hit & (col < 64)).astype(jnp.float32)
        right_imag = (hit & (col >= 64)).astype(jnp.float32)
        gram = exact_dot(exact_dot(left, real), right_real) + exact_dot(exact_dot(left, imag), right_imag)
        out[...] = jnp.broadcast_to(gram[None], out.shape)


def piece_specs(variables, points, index):
    even = pl.BlockSpec((CHIPS, variables, 16, points), lambda *at: (0, *index(*at)))
    odd = pl.BlockSpec((variables, 16, points), index)
    return [even] + [odd] * CHIPS


def gram_call(flags, pieces, weights, copies):
    part = pieces[0].shape[-1]
    count = part // CHUNK
    return pl.pallas_call(
        gram_kernel,
        grid_spec=pltpu.PrefetchScalarGridSpec(
            num_scalar_prefetch=1,
            grid=(count,),
            in_specs=[
                pl.BlockSpec((VARS, CHUNK), lambda i, flags: (0, i)),
                pl.BlockSpec((VARS, CHUNK), lambda i, flags: (0, count + i)),
                *piece_specs(VARS, CHUNK, lambda i, flags: (0, 0, i)),
            ],
            out_specs=pl.BlockSpec((copies, NB, ROWS), lambda i, flags: (0, 0, 0)),
            scratch_shapes=[pltpu.VMEM((2 * ROWS, 2 * ROWS), jnp.float32)],
        ),
        out_shape=jax.ShapeDtypeStruct((copies, NB, ROWS), jnp.float32),
        compiler_params=pltpu.CompilerParams(vmem_limit_bytes=VMEM_LIMIT),
        name="gram",
    )(flags, weights, weights, *pieces)


def coefficient_matrix(coef, chip):
    size = 2 * ROWS
    block, _, _, _ = row_facts((size, NB), 0, chip)
    left = (iota((size, NB), 1) == block).astype(jnp.bfloat16)
    rows = jnp.dot(left, coef, preferred_element_type=jnp.float32).astype(jnp.bfloat16)
    col, out = iota((ROWS, size), 0), iota((ROWS, size), 1)
    hit = (col & 63) == ((out >> 1) & 63)
    real = jnp.dot(rows, (hit & (col < 64)).astype(jnp.bfloat16), preferred_element_type=jnp.float32)
    imag = jnp.dot(rows, (hit & (col >= 64)).astype(jnp.bfloat16), preferred_element_type=jnp.float32)
    _, freq, part, half = row_facts((size, size), 0, chip)
    out = iota((size, size), 1)
    same = (freq == ((out >> 5) & 3)) & (half == (out >> 7))
    signed = jnp.where((out & 1) == 0, -imag, imag)
    full = jnp.where(same, jnp.where(part == (out & 1), real, signed), 0.0)
    return full.T.astype(jnp.bfloat16)


def modes_kernel(divisor, flags, grams, *refs):
    pieces, out, matrix = refs[:-2], refs[-2], refs[-1]

    @pl.when(pl.program_id(0) == 0)
    def _():
        coef = (jnp.sum(grams[...], 0) / divisor).astype(jnp.bfloat16)
        matrix[...] = coefficient_matrix(coef, flags[0] >> 1)

    part = pieces[0].shape[-1]
    spec = rows_of(pieces, 0)
    for start in range(0, part, CHUNK):
        modes = jnp.dot(
            matrix[...], spec[:, start : start + CHUNK], preferred_element_type=jnp.float32
        ).astype(jnp.bfloat16)
        for half in range(2):
            at = half * part + start
            rows = modes[half * ROWS : (half + 1) * ROWS]
            out[:, :, 0, :, at : at + CHUNK] = rows.reshape(OWN, NB, 2, CHUNK)


def modes_call(flags, grams, pieces, divisor):
    part = pieces[0].shape[-1]
    return pl.pallas_call(
        lambda *refs: modes_kernel(divisor, *refs),
        grid_spec=pltpu.PrefetchScalarGridSpec(
            num_scalar_prefetch=1,
            grid=(VARS,),
            in_specs=[
                pl.BlockSpec(grams.shape, lambda v, flags: (0, 0, 0)),
                *piece_specs(1, part, lambda v, flags: (v, 0, 0)),
            ],
            out_specs=pl.BlockSpec((OWN, NB, 1, 2, 2 * part), lambda v, flags: (0, 0, v, 0, 0)),
            scratch_shapes=[pltpu.VMEM((2 * ROWS, 2 * ROWS), jnp.bfloat16)],
        ),
        out_shape=jax.ShapeDtypeStruct((OWN, NB, VARS, 2, 2 * part), jnp.bfloat16),
        compiler_params=pltpu.CompilerParams(vmem_limit_bytes=VMEM_LIMIT),
        name="modes",
    )(flags, grams, *pieces)


def shifted_by(value, shift):
    pairs = [(2 * z + k, 2 * ((z + shift) % CHIPS) + k) for z in range(CHIPS) for k in range(2)]
    return lax.ppermute(value, "tm", pairs)


def shards(snapshots, tail, quad_weights):
    points = snapshots.shape[2]
    part = points // 2
    index = lax.axis_index("tm")
    record = jnp.transpose(snapshots, (1, 0, 2))
    tail = jnp.transpose(tail, (1, 0, 2))
    flags = index.astype(jnp.int32)[None]
    across = [(i, i ^ 1) for i in range(NB)]
    own = lax.dynamic_slice_in_dim(record, (index & 1) * part, part, 2)
    before = [(2 * z + 2, 2 * z) for z in range(CHIPS - 1)]
    after = [((2 * z - 1) % NB, 2 * z + 1) for z in range(CHIPS)]
    own, record = lax.optimization_barrier((own, record))
    halo = lax.ppermute(own, "tm", before + after)
    beside = lax.ppermute(record, "tm", across)
    evens = dft_even(flags, record, beside)
    evens, halo = lax.optimization_barrier((evens, halo))
    groups = [list(range(core, NB, 2)) for core in range(2)]
    evens = lax.all_to_all(evens, "tm", split_axis=0, concat_axis=0, axis_index_groups=groups, tiled=True)
    swapped = lax.ppermute(halo, "tm", across)
    odds = dft_odd(flags, record, beside, halo, swapped, tail)
    odds = [shifted_by(odd, shift) if shift else odd for odd, shift in zip(odds, SHIFTS)]
    pieces = [evens, *odds]
    slabs = lax.axis_size("pts")
    grams = gram_call(flags, pieces, quad_weights, slabs)
    grams = lax.all_to_all(grams, "pts", split_axis=0, concat_axis=0, tiled=True)
    modes = modes_call(flags, grams, pieces, float(VARS * points * slabs))
    return jnp.transpose(modes, (0, 1, 3, 2, 4))


def solution(mesh):
    placed = (P("tm", None, "pts"), P(None, None, "pts"), P(None, "pts"))
    return jax.shard_map(
        shards,
        mesh=mesh,
        in_specs=placed,
        out_specs=P("tm", None, None, None, "pts"),
        check_vma=False,
    )
```

time: 317 us -> 199 us (0.63)
  the two profiles are of different devices: /device:TPU:64 before, /device:TPU:1 now
where the time goes in v2:
time: 199 us
  waiting for transfers between devices  129 us (65%)
  starting transfers between devices  28.3 us (14%)
  Pallas kernels  17.2 us (9%)
  blocking collectives  13.2 us (7%)
  local copies, waits for them, and re-layouts  10.4 us (5%)
    ppermute x7, waiting for transfers between devices, shifted_by(): return lax.ppermute(value, 'tm', pairs)  109 us
    ppermute x7, starting transfers between devices, shifted_by(): return lax.ppermute(value, 'tm', pairs)  17.7 us
    ppermute x1, waiting for transfers between devices, shards(): halo = lax.ppermute(own, 'tm', before + after)  13.9 us
    all_to_all x1, blocking collectives, shards(): lax.all_to_all(grams, 'pts', split_axis=0, concat_axis=0, tiled=True)  13.2 us
    unnamed x16, local copies, waits for them, and re-layouts  8.71 us
    pallas_call x1, Pallas kernels, modes_call(): pl.pallas_call(lambda *refs: modes_kernel(divisor, *refs), grid_spec=pltp...  6.66 us
    all_to_all x1, starting transfers between devices, shards(): lax.all_to_all(evens, 'tm', split_axis=0, concat_axis=0, axis_index_group...  5.27 us
    pallas_call x1, Pallas kernels, gram_call(): pl.pallas_call(gram_kernel, grid_spec=pltpu.PrefetchScalarGridSpec(num_sc...  5.1 us
  transfers between devices with their start and end apart: 11, of which 8 were waited for; matrix products, arithmetic and copies ran while one was open for 0% of the time, Pallas kernels for 3%

profile of v2, /device:TPU:1, one launch (start us, length us, event | category | flops | bytes accessed | tf_op | source)
XLA Modules:
  0.0 198.8 jit_solution(8406299704703439141)
XLA Ops:
  0.0 1.7 dynamic-slice_bitcast_fusion
  2.4 3.2 %collective-permute-start = (bf16[3,64,8192]{2,1,0:T(8,128)(2,1)S(1)}, bf16[3,64,8192]{2,1,0:T(8,128)(2,1)S(1)}, u32[]{:S(2)}, u32[]{:S(2)}) collective-permute-start(bf16[3,64,8192]{2,1,0:T(8,128)(2,1)S(1)} %bitcast.6), channel_id=1, source_target_pairs={{0,1},{1,0},{2,3},{3,2},{4,5},{5,4},{6,7},{7,6},{8,9},{9,8},{10,11... | collective-permute-start | bytes 9437192 | tf_op jit(solution)/shard_map/ppermute | solution.py:284
  5.6 1.9 collective-permute-start.1
  7.5 3.4 %collective-permute-done.beside_a.beside_b = bf16[3,64,8192]{2,1,0:T(8,128)(2,1)S(1)} collective-permute-done((bf16[3,64,8192]{2,1,0:T(8,128)(2,1)S(1)}, bf16[3,64,8192]{2,1,0:T(8,128)(2,1)S(1)}, u32[]{:S(2)}, u32[]{:S(2)}) %collective-permute-start) | collective-permute-done | bytes 3145760 | tf_op jit(solution)/shard_map/ppermute | solution.py:284
  11.7 2.0 dft_even.1
  15.3 13.9 %collective-permute-done.1.halo = bf16[3,64,4096]{2,1,0:T(8,128)(2,1)} collective-permute-done((bf16[3,64,4096]{2,1,0:T(8,128)(2,1)S(1)}, bf16[3,64,4096]{2,1,0:T(8,128)(2,1)}, u32[]{:S(2)}, u32[]{:S(2)}) %collective-permute-start.1) | collective-permute-done | bytes 1572896 | tf_op jit(solution)/shard_map/ppermute | solution.py:283
  29.2 5.3 %all-to-all-start = ((bf16[8,3,16,4096]{3,2,1,0:T(8,128)(2,1)}), bf16[8,3,16,4096]{3,2,1,0:T(8,128)(2,1)}, u32[]{:S(2)}, u32[]{:S(2)}) async-start(bf16[8,3,16,4096]{3,2,1,0:T(8,128)(2,1)} %copy-done.4), calls=%async_computation | async-start | bytes 6291456 | tf_op jit(solution)/shard_map/all_to_all | solution.py:288
  34.7 3.4 %collective-permute-done.2.swapped = bf16[3,64,4096]{2,1,0:T(8,128)(2,1)S(1)} collective-permute-done((bf16[3,64,4096]{2,1,0:T(8,128)(2,1)}, bf16[3,64,4096]{2,1,0:T(8,128)(2,1)S(1)}, u32[]{:S(2)}, u32[]{:S(2)}) %collective-permute-start.2) | collective-permute-done | bytes 1572896 | tf_op jit(solution)/shard_map/ppermute | solution.py:289
  38.1 1.9 copy-done.2
  40.0 1.9 copy-done.3
  42.9 3.5 %dft_odd.1 = (bf16[3,16,4096]{2,1,0:T(8,128)(2,1)S(1)}, bf16[3,16,4096]{2,1,0:T(8,128)(2,1)S(1)}, bf16[3,16,4096]{2,1,0:T(8,128)(2,1)S(1)}, bf16[3,16,4096]{2,1,...) custom-call(s32[1]{0:T(128)} %bitcast.flags.refs_0_, ...), custom_call_target="tpu_custom_call" | custom-call | tf_op jit(solution)/shard_map/dft_odd/pallas_call | solution.py:117
  46.4 5.6 %collective-permute-start.3 = (bf16[3,16,4096]{2,1,0:T(8,128)(2,1)S(1)}, bf16[3,16,4096]{2,1,0:T(8,128)(2,1)S(1)}, u32[]{:S(2)}, u32[]{:S(2)}) collective-permute-start(bf16[3,16,4096]{2,1,0:T(8,128)(2,1)S(1)} %get-tuple-element.21), channel_id=1, source_target_pairs={{0,8},{1,9},{2,10},{3,11},{4,12},{5,13},{6,14},{7,15},{8,0},{9,1},... | collective-permute-start | bytes 1179656 | tf_op jit(solution)/shard_map/ppermute | solution.py:268
  52.2 4.2 %collective-permute-start.5 = (bf16[3,16,4096]{2,1,0:T(8,128)(2,1)S(1)}, bf16[3,16,4096]{2,1,0:T(8,128)(2,1)S(1)}, u32[]{:S(2)}, u32[]{:S(2)}) collective-permute-start(bf16[3,16,4096]{2,1,0:T(8,128)(2,1)S(1)} %get-tuple-element.23), channel_id=1, source_target_pairs={{0,10},{1,11},{2,12},{3,13},{4,14},{5,15},{6,0},{7,1},{8,2},{9,3},... | collective-permute-start | bytes 1179656 | tf_op jit(solution)/shard_map/ppermute | solution.py:268
  56.7 3.3 %collective-permute-start.7 = (bf16[3,16,4096]{2,1,0:T(8,128)(2,1)S(1)}, bf16[3,16,4096]{2,1,0:T(8,128)(2,1)S(1)}, u32[]{:S(2)}, u32[]{:S(2)}) collective-permute-start(bf16[3,16,4096]{2,1,0:T(8,128)(2,1)S(1)} %get-tuple-element.25), channel_id=1, source_target_pairs={{0,12},{1,13},{2,14},{3,15},{4,0},{5,1},{6,2},{7,3},{8,4},{9,5},{1... | collective-permute-start | bytes 1179656 | tf_op jit(solution)/shard_map/ppermute | solution.py:268
  60.0 64.0 %collective-permute-done.3.refs_1_.refs_3_ = bf16[3,16,4096]{2,1,0:T(8,128)(2,1)S(1)} collective-permute-done((bf16[3,16,4096]{2,1,0:T(8,128)(2,1)S(1)}, bf16[3,16,4096]{2,1,0:T(8,128)(2,1)S(1)}, u32[]{:S(2)}, u32[]{:S(2)}) %collective-permute-start.3) | collective-permute-done | bytes 393248 | tf_op jit(solution)/shard_map/ppermute | solution.py:268
  124.0 1.9 collective-permute-start.8
  125.9 23.0 %collective-permute-done.4.refs_2_.refs_4_ = bf16[3,16,4096]{2,1,0:T(8,128)(2,1)S(1)} collective-permute-done((bf16[3,16,4096]{2,1,0:T(8,128)(2,1)S(1)}, bf16[3,16,4096]{2,1,0:T(8,128)(2,1)S(1)}, u32[]{:S(2)}, u32[]{:S(2)}) %collective-permute-start.4) | collective-permute-done | bytes 393248 | tf_op jit(solution)/shard_map/ppermute | solution.py:268
  148.9 2.1 %collective-permute-start.9 = (bf16[3,16,4096]{2,1,0:T(8,128)(2,1)S(1)}, bf16[3,16,4096]{2,1,0:T(8,128)(2,1)S(1)}, u32[]{:S(2)}, u32[]{:S(2)}) collective-permute-start(bf16[3,16,4096]{2,1,0:T(8,128)(2,1)S(1)} %get-tuple-element.27), channel_id=1, source_target_pairs={{0,14},{1,15},{2,0},{3,1},{4,2},{5,3},{6,4},{7,5},{8,6},{9,7},{10,... | collective-permute-start | bytes 1179656 | tf_op jit(solution)/shard_map/ppermute | solution.py:268
  151.0 10.5 %collective-permute-done.6.refs_4_.refs_6_ = bf16[3,16,4096]{2,1,0:T(8,128)(2,1)S(1)} collective-permute-done((bf16[3,16,4096]{2,1,0:T(8,128)(2,1)S(1)}, bf16[3,16,4096]{2,1,0:T(8,128)(2,1)S(1)}, u32[]{:S(2)}, u32[]{:S(2)}) %collective-permute-start.6) | collective-permute-done | bytes 393248 | tf_op jit(solution)/shard_map/ppermute | solution.py:268
  161.6 2.5 %collective-permute-done.7.refs_5_.refs_7_ = bf16[3,16,4096]{2,1,0:T(8,128)(2,1)S(1)} collective-permute-done((bf16[3,16,4096]{2,1,0:T(8,128)(2,1)S(1)}, bf16[3,16,4096]{2,1,0:T(8,128)(2,1)S(1)}, u32[]{:S(2)}, u32[]{:S(2)}) %collective-permute-start.7) | collective-permute-done | bytes 393248 | tf_op jit(solution)/shard_map/ppermute | solution.py:268
  164.1 8.7 %collective-permute-done.8.refs_6_.refs_8_ = bf16[3,16,4096]{2,1,0:T(8,128)(2,1)S(1)} collective-permute-done((bf16[3,16,4096]{2,1,0:T(8,128)(2,1)S(1)}, bf16[3,16,4096]{2,1,0:T(8,128)(2,1)S(1)}, u32[]{:S(2)}, u32[]{:S(2)}) %collective-permute-start.8) | collective-permute-done | bytes 393248 | tf_op jit(solution)/shard_map/ppermute | solution.py:268
  173.7 5.1 %gram.1 = f32[16,16,128]{2,1,0:T(8,128)S(1)} custom-call(s32[1]{0:T(128)} %bitcast.flags.refs_0_, f32[3,8192]{1,0:T(4,128)S(1)} %copy-done.5, f32[3,8192]{1,0:T(4,128)S(1)} %copy-done.5, bf16[8,3,16,4096]{3,2,1,0:T(8,128)(2,1)} %all-to-all-done.refs_0_.refs_2_, bf16[3,16,4096]{2,1,0:T(8,128)(2,1)S(1)} %collective-permute-done.3.refs_1_.refs_3_, ...), custom_call_target="tpu_custom_call" | custom-call | tf_op jit(solution)/shard_map/gram/pallas_call | solution.py:190
  178.9 13.2 %all_to_all.10.refs_1_ = f32[16,16,128]{2,1,0:T(8,128)S(1)} all-to-all(f32[16,16,128]{2,1,0:T(8,128)S(1)} %gram.1), channel_id=1, replica_groups=mesh['pts'=16,'tm'=16] {'pts'}, dimensions={0} | all-to-all | bytes 262144 | tf_op jit(solution)/shard_map/all_to_all | solution.py:295
  192.1 6.7 %modes.1 = bf16[4,16,3,2,8192]{4,3,2,1,0:T(2,128)(2,1)} custom-call(s32[1]{0:T(128)} %bitcast.flags.refs_0_, f32[16,16,128]{2,1,0:T(8,128)S(1)} %all_to_all.10.refs_1_, bf16[8,3,16,4096]{3,2,1,0:T(8,128)(2,1)} %all-to-all-done.refs_0_.refs_2_, bf16[3,16,4096]{2,1,0:T(8,128)(2,1)S(1)} %collective-permute-done.3.refs_1_.refs_3_, ...), custom_call_target="tpu_custom_call" | custom-call | tf_op jit(solution)/shard_map/modes/pallas_call | solution.py:248
  (20 shorter events, 5.7 us)
Async XLA Ops:
  0.0 2.4 %copy-start = (bf16[64,3,8192]{2,0,1:T(8,128)(2,1)S(1)}, bf16[64,3,8192]{2,0,1:T(8,128)(2,1)}, u32[]{:S(2)}) copy-start(bf16[64,3,8192]{2,0,1:T(8,128)(2,1)} %param.5) | copy-start | bytes 9437188
  2.4 8.5 %collective-permute-start = (bf16[3,64,8192]{2,1,0:T(8,128)(2,1)S(1)}, bf16[3,64,8192]{2,1,0:T(8,128)(2,1)S(1)}, u32[]{:S(2)}, u32[]{:S(2)}) collective-permute-start(bf16[3,64,8192]{2,1,0:T(8,128)(2,1)S(1)} %bitcast.6), channel_id=1, source_target_pairs={{0,1},{1,0},{2,3},{3,2},{4,5},{5,4},{6,7},{7,6},{8,9},{9,8},{10,11... | collective-permute-start | bytes 9437192 | tf_op jit(solution)/shard_map/ppermute | solution.py:284
  5.6 23.6 %collective-permute-start.1 = (bf16[3,64,4096]{2,1,0:T(8,128)(2,1)S(1)}, bf16[3,64,4096]{2,1,0:T(8,128)(2,1)}, u32[]{:S(2)}, u32[]{:S(2)}) collective-permute-start(bf16[3,64,4096]{2,1,0:T(8,128)(2,1)S(1)} %dynamic-slice_bitcast_fusion), channel_id=1, source_target_pairs={{2,0},{4,2},{6,4},{8,6},{10,8},{12,10},{14,12},{15,1},{1,3},{3,5},... | collective-permute-start | bytes 4718600 | tf_op jit(solution)/shard_map/ppermute | solution.py:283
  10.9 2.7 %copy-start.1 = (bf16[3,64,8192]{2,1,0:T(8,128)(2,1)}, bf16[3,64,8192]{2,1,0:T(8,128)(2,1)S(1)}, u32[]{:S(2)}) copy-start(bf16[3,64,8192]{2,1,0:T(8,128)(2,1)S(1)} %collective-permute-done.beside_a.beside_b) | copy-start | bytes 9437188
  10.9 0.8 copy-start.7
  13.6 1.7 copy-start.4
  29.2 143.6 %all-to-all-start = ((bf16[8,3,16,4096]{3,2,1,0:T(8,128)(2,1)}), bf16[8,3,16,4096]{3,2,1,0:T(8,128)(2,1)}, u32[]{:S(2)}, u32[]{:S(2)}) async-start(bf16[8,3,16,4096]{3,2,1,0:T(8,128)(2,1)} %copy-done.4), calls=%async_computation | async-start | bytes 6291456 | tf_op jit(solution)/shard_map/all_to_all | solution.py:288
  34.5 3.6 %collective-permute-start.2 = (bf16[3,64,4096]{2,1,0:T(8,128)(2,1)}, bf16[3,64,4096]{2,1,0:T(8,128)(2,1)S(1)}, u32[]{:S(2)}, u32[]{:S(2)}) collective-permute-start(bf16[3,64,4096]{2,1,0:T(8,128)(2,1)} %collective-permute-done.1.halo), channel_id=1, source_target_pairs={{0,1},{1,0},{2,3},{3,2},{4,5},{5,4},{6,7},{7,6},{8,9},{9,8},{10,11... | collective-permute-start | bytes 4718600 | tf_op jit(solution)/shard_map/ppermute | solution.py:289
  38.1 1.9 copy-start.2
  40.0 1.9 copy-start.3
  41.9 0.9 copy-start.6
  46.4 77.6 %collective-permute-start.3 = (bf16[3,16,4096]{2,1,0:T(8,128)(2,1)S(1)}, bf16[3,16,4096]{2,1,0:T(8,128)(2,1)S(1)}, u32[]{:S(2)}, u32[]{:S(2)}) collective-permute-start(bf16[3,16,4096]{2,1,0:T(8,128)(2,1)S(1)} %get-tuple-element.21), channel_id=1, source_target_pairs={{0,8},{1,9},{2,10},{3,11},{4,12},{5,13},{6,14},{7,15},{8,0},{9,1},... | collective-permute-start | bytes 1179656 | tf_op jit(solution)/shard_map/ppermute | solution.py:268
  52.0 96.9 %collective-permute-start.4 = (bf16[3,16,4096]{2,1,0:T(8,128)(2,1)S(1)}, bf16[3,16,4096]{2,1,0:T(8,128)(2,1)S(1)}, u32[]{:S(2)}, u32[]{:S(2)}) collective-permute-start(bf16[3,16,4096]{2,1,0:T(8,128)(2,1)S(1)} %get-tuple-element.22), channel_id=1, source_target_pairs={{0,6},{1,7},{2,8},{3,9},{4,10},{5,11},{6,12},{7,13},{8,14},{9,15},... | collective-permute-start | bytes 1179656 | tf_op jit(solution)/shard_map/ppermute | solution.py:268
  52.2 98.8 %collective-permute-start.5 = (bf16[3,16,4096]{2,1,0:T(8,128)(2,1)S(1)}, bf16[3,16,4096]{2,1,0:T(8,128)(2,1)S(1)}, u32[]{:S(2)}, u32[]{:S(2)}) collective-permute-start(bf16[3,16,4096]{2,1,0:T(8,128)(2,1)S(1)} %get-tuple-element.23), channel_id=1, source_target_pairs={{0,10},{1,11},{2,12},{3,13},{4,14},{5,15},{6,0},{7,1},{8,2},{9,3},... | collective-permute-start | bytes 1179656 | tf_op jit(solution)/shard_map/ppermute | solution.py:268
  56.4 105.1 %collective-permute-start.6 = (bf16[3,16,4096]{2,1,0:T(8,128)(2,1)S(1)}, bf16[3,16,4096]{2,1,0:T(8,128)(2,1)S(1)}, u32[]{:S(2)}, u32[]{:S(2)}) collective-permute-start(bf16[3,16,4096]{2,1,0:T(8,128)(2,1)S(1)} %get-tuple-element.24), channel_id=1, source_target_pairs={{0,4},{1,5},{2,6},{3,7},{4,8},{5,9},{6,10},{7,11},{8,12},{9,13},{1... | collective-permute-start | bytes 1179656 | tf_op jit(solution)/shard_map/ppermute | solution.py:268
  56.7 107.4 %collective-permute-start.7 = (bf16[3,16,4096]{2,1,0:T(8,128)(2,1)S(1)}, bf16[3,16,4096]{2,1,0:T(8,128)(2,1)S(1)}, u32[]{:S(2)}, u32[]{:S(2)}) collective-permute-start(bf16[3,16,4096]{2,1,0:T(8,128)(2,1)S(1)} %get-tuple-element.25), channel_id=1, source_target_pairs={{0,12},{1,13},{2,14},{3,15},{4,0},{5,1},{6,2},{7,3},{8,4},{9,5},{1... | collective-permute-start | bytes 1179656 | tf_op jit(solution)/shard_map/ppermute | solution.py:268
  124.0 48.9 %collective-permute-start.8 = (bf16[3,16,4096]{2,1,0:T(8,128)(2,1)S(1)}, bf16[3,16,4096]{2,1,0:T(8,128)(2,1)S(1)}, u32[]{:S(2)}, u32[]{:S(2)}) collective-permute-start(bf16[3,16,4096]{2,1,0:T(8,128)(2,1)S(1)} %get-tuple-element.26), channel_id=1, source_target_pairs={{0,2},{1,3},{2,4},{3,5},{4,6},{5,7},{6,8},{7,9},{8,10},{9,11},{10,... | collective-permute-start | bytes 1179656 | tf_op jit(solution)/shard_map/ppermute | solution.py:268
  148.9 23.9 %collective-permute-start.9 = (bf16[3,16,4096]{2,1,0:T(8,128)(2,1)S(1)}, bf16[3,16,4096]{2,1,0:T(8,128)(2,1)S(1)}, u32[]{:S(2)}, u32[]{:S(2)}) collective-permute-start(bf16[3,16,4096]{2,1,0:T(8,128)(2,1)S(1)} %get-tuple-element.27), channel_id=1, source_target_pairs={{0,14},{1,15},{2,0},{3,1},{4,2},{5,3},{6,4},{7,5},{8,6},{9,7},{10,... | collective-permute-start | bytes 1179656 | tf_op jit(solution)/shard_map/ppermute | solution.py:268
  172.8 0.9 copy-start.5

commit v3 on v2

--- a/solution.py
+++ b/solution.py
@@ -16,7 +16,9 @@
 OWN = 4
 CHIPS = 8
 ROWS = 128
-CHUNK = 1024
+CHUNK = 2048
+COVER = 30_000_000_000
+HELD = 6
 WIDE = 4096
 VMEM_LIMIT = 28 * 1024 * 1024
 SHIFTS = (4, 3, 5, 2, 6, 1, 7, 0)
@@ -123,18 +125,49 @@
             out_specs=[low_out] * CHIPS,
         ),
         out_shape=[jax.ShapeDtypeStruct((VARS, 16, part), jnp.bfloat16)] * CHIPS,
+        cost_estimate=pl.CostEstimate(flops=COVER, bytes_accessed=COVER, transcendentals=0),
         compiler_params=pltpu.CompilerParams(vmem_limit_bytes=VMEM_LIMIT),
         name="dft_odd",
     )(flags, jnp.asarray(table), record, record, beside, beside, halo, swapped, tail, tail)
 
 
-def exact_dot(left, right):
-    return jnp.dot(left, right, precision=lax.Precision.HIGHEST, preferred_element_type=jnp.float32)
+def selected(chosen, values, from_left):
+    result = None
+    for _ in range(3):
+        term = values.astype(jnp.bfloat16)
+        values = values - term.astype(jnp.float32)
+        pair = (chosen, term) if from_left else (term, chosen)
+        product = jnp.dot(*pair, preferred_element_type=jnp.float32)
+        result = product if result is None else result + product
+    return result
 
 
 def rows_of(pieces, v):
     evens = pieces[0][:, v].reshape(ROWS, pieces[0].shape[-1])
     return jnp.concatenate([evens, *(piece[v] for piece in pieces[1:])], 0)
+
+
+def held_kernel(evens, weights, evens_out, weights_out):
+    evens_out[...] = evens[...]
+    weights_out[...] = weights[...]
+
+
+def held_call(evens, weights):
+    part = evens.shape[-1]
+    piece = pl.BlockSpec((1, VARS, 16, part), lambda i: (i, 0, 0, 0))
+    line = pl.BlockSpec(weights.shape, lambda i: (0, 0))
+    return pl.pallas_call(
+        held_kernel,
+        grid=(CHIPS,),
+        in_specs=[piece, line],
+        out_specs=[piece, line],
+        out_shape=[
+            jax.ShapeDtypeStruct(evens.shape, evens.dtype),
+            jax.ShapeDtypeStruct(weights.shape, weights.dtype),
+        ],
+        compiler_params=pltpu.CompilerParams(vmem_limit_bytes=VMEM_LIMIT),
+        name="held",
+    )(evens, weights)
 
 
 def gram_kernel(flags, weights_a, weights_b, *refs):
@@ -161,20 +194,19 @@
     @pl.when(step == pl.num_programs(0) - 1)
     def _():
         chip = flags[0] >> 1
-        _, freq_i, part_i, half_i = row_facts((size, size), 0, chip)
-        _, freq_j, part_j, half_j = row_facts((size, size), 1, chip)
-        same = (freq_i == freq_j) & (half_i == half_j)
         sums = total[...]
-        real = jnp.where(same & (part_i == part_j), sums, 0.0)
-        imag = jnp.where(same & (part_i != part_j), jnp.where(part_i == 0, sums, -sums), 0.0)
+        mixed = iota((size, size), 0) ^ iota((size, size), 1)
+        same = (mixed & 14) == 0
+        signed = jnp.where((iota((size, size), 0) & 1) == 0, sums, -sums)
+        equal, other = same & ((mixed & 1) == 0), same & ((mixed & 1) == 1)
+        masked = jnp.concatenate([jnp.where(equal, sums, 0.0), jnp.where(other, signed, 0.0)], 1)
         block, _, _, _ = row_facts((NB, size), 1, chip)
-        left = (iota((NB, size), 0) == block).astype(jnp.float32)
+        left = (iota((NB, size), 0) == block).astype(jnp.bfloat16)
         block, freq, _, _ = row_facts((size, ROWS), 0, chip)
         col = iota((size, ROWS), 1)
         hit = (block == (col & 15)) & (freq == ((col >> 4) & 3))
-        right_real = (hit & (col < 64)).astype(jnp.float32)
-        right_imag = (hit & (col >= 64)).astype(jnp.float32)
-        gram = exact_dot(exact_dot(left, real), right_real) + exact_dot(exact_dot(left, imag), right_imag)
+        right = jnp.concatenate([hit & (col < 64), hit & (col >= 64)], 0).astype(jnp.bfloat16)
+        gram = selected(right, selected(left, masked, True), False)
         out[...] = jnp.broadcast_to(gram[None], out.shape)
 
 
@@ -283,11 +315,12 @@
     halo = lax.ppermute(own, "tm", before + after)
     beside = lax.ppermute(record, "tm", across)
     evens = dft_even(flags, record, beside)
-    evens, halo = lax.optimization_barrier((evens, halo))
     groups = [list(range(core, NB, 2)) for core in range(2)]
     evens = lax.all_to_all(evens, "tm", split_axis=0, concat_axis=0, axis_index_groups=groups, tiled=True)
     swapped = lax.ppermute(halo, "tm", across)
-    odds = dft_odd(flags, record, beside, halo, swapped, tail)
+    odds = [*dft_odd(flags, record, beside, halo, swapped, tail)]
+    evens, quad_weights = held_call(evens, quad_weights)
+    evens, quad_weights, odds[HELD] = lax.optimization_barrier((evens, quad_weights, odds[HELD]))
     odds = [shifted_by(odd, shift) if shift else odd for odd, shift in zip(odds, SHIFTS)]
     pieces = [evens, *odds]
     slabs = lax.axis_size("pts")

time: 199 us -> 187 us (0.940)
  waiting for transfers between devices: 129 us -> 97.2 us
  starting transfers between devices: 28.3 us -> 42.5 us
  local copies, waits for them, and re-layouts: 10.4 us -> 14.2 us
    ppermute x7, waiting for transfers between devices: 109 us -> 47.3 us  [shifted_by(): return lax.ppermute(value, 'tm', pairs)]
    all_to_all x1, waiting for transfers between devices: 0.01 us -> 34.3 us  [shards(): lax.all_to_all(evens, 'tm', split_axis=0, concat_axis=0, axis_index_group...]
    ppermute x7, starting transfers between devices: 17.7 us -> 30.9 us  [shifted_by(): return lax.ppermute(value, 'tm', pairs)]
    ppermute x1, waiting for transfers between devices: 13.9 us -> 8.65 us  [shards(): halo = lax.ppermute(own, 'tm', before + after)]
    pallas_call x0 -> x1, Pallas kernels: none -> 4.43 us  [held_call(): pl.pallas_call(held_kernel, grid=(CHIPS,), in_specs=[piece, line], out_sp...]
    unnamed x16 -> x24, local copies, waits for them, and re-layouts: 8.71 us -> 11.3 us
  transfers between devices with their start and end apart: 11 -> 11, of which waited for: 8 -> 8; matrix products, arithmetic and copies ran while one was open for 0% -> 0% of each run, Pallas kernels for 3% -> 6%
where the time goes in v3:
time: 187 us; the launch traced here: 186 us
  waiting for transfers between devices  97.2 us (52%)
  starting transfers between devices  42.5 us (23%)
  Pallas kernels  18.8 us (10%)
  local copies, waits for them, and re-layouts  14.2 us (8%)
  blocking collectives  13.6 us (7%)
    ppermute x7, waiting for transfers between devices, shifted_by(): return lax.ppermute(value, 'tm', pairs)  47.3 us
    all_to_all x1, waiting for transfers between devices, shards(): lax.all_to_all(evens, 'tm', split_axis=0, concat_axis=0, axis_index_group...  34.3 us
    ppermute x7, starting transfers between devices, shifted_by(): return lax.ppermute(value, 'tm', pairs)  30.9 us
    all_to_all x1, blocking collectives, shards(): lax.all_to_all(grams, 'pts', split_axis=0, concat_axis=0, tiled=True)  13.6 us
    unnamed x24, local copies, waits for them, and re-layouts  11.3 us
    ppermute x1, waiting for transfers between devices, shards(): halo = lax.ppermute(own, 'tm', before + after)  8.65 us
    all_to_all x1, starting transfers between devices, shards(): lax.all_to_all(evens, 'tm', split_axis=0, concat_axis=0, axis_index_group...  6.45 us
    pallas_call x1, Pallas kernels, modes_call(): pl.pallas_call(lambda *refs: modes_kernel(divisor, *refs), grid_spec=pltp...  4.87 us
  transfers between devices with their start and end apart: 11, of which 8 were waited for; matrix products, arithmetic and copies ran while one was open for 0% of the time, Pallas kernels for 6%

profile of v3, /device:TPU:1, one launch (start us, length us, event | category | flops | bytes accessed | tf_op | source)
XLA Modules:
  0.0 186.5 jit_solution(14508305211055509574)
XLA Ops:
  0.0 3.0 %dynamic-slice_bitcast_fusion = bf16[3,64,4096]{2,1,0:T(8,128)(2,1)} fusion(bf16[64,3,8192]{2,0,1:T(8,128)(2,1)} %param.5, s32[]{:T(128)S(6)} %select_n.3), kind=kLoop, calls=%fused_computation | loop fusion | bytes 3145732 | tf_op jit(solution)/shard_map/dynamic_slice | solution.py:311
  3.0 3.2 %collective-permute-start = (bf16[3,64,8192]{2,1,0:T(8,128)(2,1)S(1)}, bf16[3,64,8192]{2,1,0:T(8,128)(2,1)S(1)}, u32[]{:S(2)}, u32[]{:S(2)}) collective-permute-start(bf16[3,64,8192]{2,1,0:T(8,128)(2,1)S(1)} %bitcast.6), channel_id=1, source_target_pairs={{0,1},{1,0},{2,3},{3,2},{4,5},{5,4},{6,7},{7,6},{8,9},{9,8},{10,11... | collective-permute-start | bytes 9437192 | tf_op jit(solution)/shard_map/ppermute | solution.py:316
  6.2 1.9 %collective-permute-start.1 = (bf16[3,64,4096]{2,1,0:T(8,128)(2,1)}, bf16[3,64,4096]{2,1,0:T(8,128)(2,1)}, u32[]{:S(2)}, u32[]{:S(2)}) collective-permute-start(bf16[3,64,4096]{2,1,0:T(8,128)(2,1)} %dynamic-slice_bitcast_fusion), channel_id=1, source_target_pairs={{2,0},{4,2},{6,4},{8,6},{10,8},{12,10},{14,12},{15,1},{1,3},{3,5},... | collective-permute-start | bytes 4718600 | tf_op jit(solution)/shard_map/ppermute | solution.py:315
  8.1 3.4 %collective-permute-done.beside_a.beside_b = bf16[3,64,8192]{2,1,0:T(8,128)(2,1)S(1)} collective-permute-done((bf16[3,64,8192]{2,1,0:T(8,128)(2,1)S(1)}, bf16[3,64,8192]{2,1,0:T(8,128)(2,1)S(1)}, u32[]{:S(2)}, u32[]{:S(2)}) %collective-permute-start) | collective-permute-done | bytes 3145760 | tf_op jit(solution)/shard_map/ppermute | solution.py:316
  12.3 2.0 %dft_even.1 = bf16[8,3,16,4096]{3,2,1,0:T(8,128)(2,1)S(1)} custom-call(s32[1]{0:T(128)} %bitcast.flags.refs_0_, bf16[2,64,128]{2,1,0:T(8,128)(2,1)S(1)} %copy-done.5, bf16[3,64,8192]{2,1,0:T(8,128)(2,1)S(1)} %bitcast.7, bf16[3,64,8192]{2,1,0:T(8,128)(2,1)S(1)} %bitcast.8, bf16[3,64,8192]{2,1,0:T(8,128)(2,1)S(1)} %collective-permute-done.beside_a.beside_b, ...), custom_call_target="tpu_custom_call" | custom-call | tf_op jit(solution)/shard_map/dft_even/pallas_call | solution.py:72
  17.6 6.4 %all-to-all-start = ((bf16[8,3,16,4096]{3,2,1,0:T(8,128)(2,1)}), bf16[8,3,16,4096]{3,2,1,0:T(8,128)(2,1)}, u32[]{:S(2)}, u32[]{:S(2)}) async-start(bf16[8,3,16,4096]{3,2,1,0:T(8,128)(2,1)} %copy-done.1), calls=%async_computation | async-start | bytes 6291456 | tf_op jit(solution)/shard_map/all_to_all | solution.py:319
  24.0 8.6 %collective-permute-done.1.halo = bf16[3,64,4096]{2,1,0:T(8,128)(2,1)} collective-permute-done((bf16[3,64,4096]{2,1,0:T(8,128)(2,1)}, bf16[3,64,4096]{2,1,0:T(8,128)(2,1)}, u32[]{:S(2)}, u32[]{:S(2)}) %collective-permute-start.1) | collective-permute-done | bytes 1572896 | tf_op jit(solution)/shard_map/ppermute | solution.py:315
  32.7 3.6 %collective-permute-done.2.swapped = bf16[3,64,4096]{2,1,0:T(8,128)(2,1)S(1)} collective-permute-done((bf16[3,64,4096]{2,1,0:T(8,128)(2,1)}, bf16[3,64,4096]{2,1,0:T(8,128)(2,1)S(1)}, u32[]{:S(2)}, u32[]{:S(2)}) %collective-permute-start.2) | collective-permute-done | bytes 1572896 | tf_op jit(solution)/shard_map/ppermute | solution.py:320
  36.3 1.9 %copy-done.3 = bf16[3,64,8192]{2,1,0:T(8,128)(2,1)S(1)} copy-done((bf16[3,64,8192]{2,1,0:T(8,128)(2,1)S(1)}, bf16[3,64,8192]{2,1,0:T(8,128)(2,1)}, u32[]{:S(2)}) %copy-start.3) | copy-done | bytes 3145752
  38.2 1.9 %copy-done.6 = bf16[64,3,8192]{2,0,1:T(8,128)(2,1)S(1)} copy-done((bf16[64,3,8192]{2,0,1:T(8,128)(2,1)S(1)}, bf16[64,3,8192]{2,0,1:T(8,128)(2,1)}, u32[]{:S(2)}) %copy-start.6) | copy-done | bytes 3145752
  41.0 4.4 %dft_odd.1 = (bf16[3,16,4096]{2,1,0:T(8,128)(2,1)}, bf16[3,16,4096]{2,1,0:T(8,128)(2,1)}, bf16[3,16,4096]{2,1,0:T(8,128)(2,1)}, bf16[3,16,4096]{2,1,0:T(8,128)(2...) custom-call(s32[1]{0:T(128)} %bitcast.flags.refs_0_, ...), custom_call_target="tpu_custom_call" | custom-call | flops 30000001024 | bytes 30000001024 | tf_op jit(solution)/shard_map/dft_odd/pallas_call | solution.py:119
  46.9 4.5 %collective-permute-start.3 = (bf16[3,16,4096]{2,1,0:T(8,128)(2,1)}, bf16[3,16,4096]{2,1,0:T(8,128)(2,1)S(1)}, u32[]{:S(2)}, u32[]{:S(2)}) collective-permute-start(bf16[3,16,4096]{2,1,0:T(8,128)(2,1)} %get-tuple-element.27), channel_id=1, source_target_pairs={{0,8},{1,9},{2,10},{3,11},{4,12},{5,13},{6,14},{7,15},{8,0},{9,1},... | collective-permute-start | bytes 1179656 | tf_op jit(solution)/shard_map/ppermute | solution.py:300
  51.5 4.4 %collective-permute-start.5 = (bf16[3,16,4096]{2,1,0:T(8,128)(2,1)}, bf16[3,16,4096]{2,1,0:T(8,128)(2,1)S(1)}, u32[]{:S(2)}, u32[]{:S(2)}) collective-permute-start(bf16[3,16,4096]{2,1,0:T(8,128)(2,1)} %get-tuple-element.29), channel_id=1, source_target_pairs={{0,10},{1,11},{2,12},{3,13},{4,14},{5,15},{6,0},{7,1},{8,2},{9,3},... | collective-permute-start | bytes 1179656 | tf_op jit(solution)/shard_map/ppermute | solution.py:300
  56.8 2.7 %collective-permute-start.7 = (bf16[3,16,4096]{2,1,0:T(8,128)(2,1)}, bf16[3,16,4096]{2,1,0:T(8,128)(2,1)S(1)}, u32[]{:S(2)}, u32[]{:S(2)}) collective-permute-start(bf16[3,16,4096]{2,1,0:T(8,128)(2,1)} %get-tuple-element.31), channel_id=1, source_target_pairs={{0,12},{1,13},{2,14},{3,15},{4,0},{5,1},{6,2},{7,3},{8,4},{9,5},{1... | collective-permute-start | bytes 1179656 | tf_op jit(solution)/shard_map/ppermute | solution.py:300
  59.5 34.3 %all-to-all-done.evens = bf16[8,3,16,4096]{3,2,1,0:T(8,128)(2,1)} async-done(((bf16[8,3,16,4096]{3,2,1,0:T(8,128)(2,1)}), bf16[8,3,16,4096]{3,2,1,0:T(8,128)(2,1)}, u32[]{:S(2)}, u32[]{:S(2)}) %all-to-all-start) | async-done | bytes 3145760 | tf_op jit(solution)/shard_map/all_to_all | solution.py:319
  94.7 4.4 %held.1 = (bf16[8,3,16,4096]{3,2,1,0:T(8,128)(2,1)S(1)}, f32[3,8192]{1,0:T(4,128)S(1)}) custom-call(bf16[8,3,16,4096]{3,2,1,0:T(8,128)(2,1)} %all-to-all-done.evens, f32[3,8192]{1,0:T(4,128)S(1)} %copy-done.4), custom_call_target="tpu_custom_call" | custom-call | tf_op jit(solution)/shard_map/held/pallas_call | solution.py:159
  99.1 5.3 %collective-permute-done.3.refs_1_.refs_3_ = bf16[3,16,4096]{2,1,0:T(8,128)(2,1)S(1)} collective-permute-done((bf16[3,16,4096]{2,1,0:T(8,128)(2,1)}, bf16[3,16,4096]{2,1,0:T(8,128)(2,1)S(1)}, u32[]{:S(2)}, u32[]{:S(2)}) %collective-permute-start.3) | collective-permute-done | bytes 393248 | tf_op jit(solution)/shard_map/ppermute | solution.py:300
  104.4 18.4 %collective-permute-start.8 = (bf16[3,16,4096]{2,1,0:T(8,128)(2,1)S(1)}, bf16[3,16,4096]{2,1,0:T(8,128)(2,1)S(1)}, u32[]{:S(2)}, u32[]{:S(2)}) collective-permute-start(bf16[3,16,4096]{2,1,0:T(8,128)(2,1)S(1)} %copy-done.10), channel_id=1, source_target_pairs={{0,2},{1,3},{2,4},{3,5},{4,6},{5,7},{6,8},{7,9},{8,10},{9,11},{10,... | collective-permute-start | bytes 1179656 | tf_op jit(solution)/shard_map/ppermute | solution.py:300
  122.8 22.0 %collective-permute-done.4.refs_2_.refs_4_ = bf16[3,16,4096]{2,1,0:T(8,128)(2,1)S(1)} collective-permute-done((bf16[3,16,4096]{2,1,0:T(8,128)(2,1)}, bf16[3,16,4096]{2,1,0:T(8,128)(2,1)S(1)}, u32[]{:S(2)}, u32[]{:S(2)}) %collective-permute-start.4) | collective-permute-done | bytes 393248 | tf_op jit(solution)/shard_map/ppermute | solution.py:300
  144.8 13.9 %collective-permute-done.6.refs_4_.refs_6_ = bf16[3,16,4096]{2,1,0:T(8,128)(2,1)S(1)} collective-permute-done((bf16[3,16,4096]{2,1,0:T(8,128)(2,1)}, bf16[3,16,4096]{2,1,0:T(8,128)(2,1)S(1)}, u32[]{:S(2)}, u32[]{:S(2)}) %collective-permute-start.6) | collective-permute-done | bytes 393248 | tf_op jit(solution)/shard_map/ppermute | solution.py:300
  158.7 6.1 %collective-permute-done.8.refs_6_.refs_8_ = bf16[3,16,4096]{2,1,0:T(8,128)(2,1)S(1)} collective-permute-done((bf16[3,16,4096]{2,1,0:T(8,128)(2,1)S(1)}, bf16[3,16,4096]{2,1,0:T(8,128)(2,1)S(1)}, u32[]{:S(2)}, u32[]{:S(2)}) %collective-permute-start.8) | collective-permute-done | bytes 393248 | tf_op jit(solution)/shard_map/ppermute | solution.py:300
  164.8 3.2 %gram.1 = f32[16,16,128]{2,1,0:T(8,128)S(1)} custom-call(s32[1]{0:T(128)} %bitcast.flags.refs_0_, f32[3,8192]{1,0:T(4,128)S(1)} %get-tuple-element.25.weights_a.weights_b, f32[3,8192]{1,0:T(4,128)S(1)} %get-tuple-element.25.weights_a.weights_b, bf16[8,3,16,4096]{3,2,1,0:T(8,128)(2,1)S(1)} %get-tuple-element.26.refs_0_.refs_2_, ...), custom_call_target="tpu_custom_call" | custom-call | tf_op jit(solution)/shard_map/gram/pallas_call | solution.py:222
  168.0 13.6 %all_to_all.10.refs_1_ = f32[16,16,128]{2,1,0:T(8,128)S(1)} all-to-all(f32[16,16,128]{2,1,0:T(8,128)S(1)} %gram.1), channel_id=1, replica_groups=mesh['pts'=16,'tm'=16] {'pts'}, dimensions={0} | all-to-all | bytes 262144 | tf_op jit(solution)/shard_map/all_to_all | solution.py:328
  181.6 4.9 %modes.1 = bf16[4,16,3,2,8192]{4,3,2,1,0:T(2,128)(2,1)} custom-call(s32[1]{0:T(128)} %bitcast.flags.refs_0_, f32[16,16,128]{2,1,0:T(8,128)S(1)} %all_to_all.10.refs_1_, bf16[8,3,16,4096]{3,2,1,0:T(8,128)(2,1)S(1)} %get-tuple-element.26.refs_0_.refs_2_, bf16[3,16,4096]{2,1,0:T(8,128)(2,1)S(1)} %collective-permute-done.3.refs_1_.refs_3_, ...), custom_call_target="tpu_custom_call" | custom-call | tf_op jit(solution)/shard_map/modes/pallas_call | solution.py:280
  (29 shorter events, 8.5 us)
Async XLA Ops:
  0.0 3.0 %copy-start = (bf16[64,3,8192]{2,0,1:T(8,128)(2,1)S(1)}, bf16[64,3,8192]{2,0,1:T(8,128)(2,1)}, u32[]{:S(2)}) copy-start(bf16[64,3,8192]{2,0,1:T(8,128)(2,1)} %param.5) | copy-start | bytes 9437188
  3.0 8.5 %collective-permute-start = (bf16[3,64,8192]{2,1,0:T(8,128)(2,1)S(1)}, bf16[3,64,8192]{2,1,0:T(8,128)(2,1)S(1)}, u32[]{:S(2)}, u32[]{:S(2)}) collective-permute-start(bf16[3,64,8192]{2,1,0:T(8,128)(2,1)S(1)} %bitcast.6), channel_id=1, source_target_pairs={{0,1},{1,0},{2,3},{3,2},{4,5},{5,4},{6,7},{7,6},{8,9},{9,8},{10,11... | collective-permute-start | bytes 9437192 | tf_op jit(solution)/shard_map/ppermute | solution.py:316
  6.2 26.4 %collective-permute-start.1 = (bf16[3,64,4096]{2,1,0:T(8,128)(2,1)}, bf16[3,64,4096]{2,1,0:T(8,128)(2,1)}, u32[]{:S(2)}, u32[]{:S(2)}) collective-permute-start(bf16[3,64,4096]{2,1,0:T(8,128)(2,1)} %dynamic-slice_bitcast_fusion), channel_id=1, source_target_pairs={{2,0},{4,2},{6,4},{8,6},{10,8},{12,10},{14,12},{15,1},{1,3},{3,5},... | collective-permute-start | bytes 4718600 | tf_op jit(solution)/shard_map/ppermute | solution.py:315
  11.5 0.8 copy-start.5
  14.2 1.7 copy-start.1
  15.9 1.7 copy-start.2
  17.6 76.2 %all-to-all-start = ((bf16[8,3,16,4096]{3,2,1,0:T(8,128)(2,1)}), bf16[8,3,16,4096]{3,2,1,0:T(8,128)(2,1)}, u32[]{:S(2)}, u32[]{:S(2)}) async-start(bf16[8,3,16,4096]{3,2,1,0:T(8,128)(2,1)} %copy-done.1), calls=%async_computation | async-start | bytes 6291456 | tf_op jit(solution)/shard_map/all_to_all | solution.py:319
  32.7 3.6 %collective-permute-start.2 = (bf16[3,64,4096]{2,1,0:T(8,128)(2,1)}, bf16[3,64,4096]{2,1,0:T(8,128)(2,1)S(1)}, u32[]{:S(2)}, u32[]{:S(2)}) collective-permute-start(bf16[3,64,4096]{2,1,0:T(8,128)(2,1)} %collective-permute-done.1.halo), channel_id=1, source_target_pairs={{0,1},{1,0},{2,3},{3,2},{4,5},{5,4},{6,7},{7,6},{8,9},{9,8},{10,11... | collective-permute-start | bytes 4718600 | tf_op jit(solution)/shard_map/ppermute | solution.py:320
  36.3 1.9 %copy-start.3 = (bf16[3,64,8192]{2,1,0:T(8,128)(2,1)S(1)}, bf16[3,64,8192]{2,1,0:T(8,128)(2,1)}, u32[]{:S(2)}) copy-start(bf16[3,64,8192]{2,1,0:T(8,128)(2,1)} %copy-done.2) | copy-start | bytes 9437188
  38.2 1.9 %copy-start.6 = (bf16[64,3,8192]{2,0,1:T(8,128)(2,1)S(1)}, bf16[64,3,8192]{2,0,1:T(8,128)(2,1)}, u32[]{:S(2)}) copy-start(bf16[64,3,8192]{2,0,1:T(8,128)(2,1)} %param.6) | copy-start | bytes 9437188
  40.1 0.9 copy-start.11
  45.4 0.8 copy-start.7
  46.2 0.8 copy-start.9
  46.9 57.5 %collective-permute-start.3 = (bf16[3,16,4096]{2,1,0:T(8,128)(2,1)}, bf16[3,16,4096]{2,1,0:T(8,128)(2,1)S(1)}, u32[]{:S(2)}, u32[]{:S(2)}) collective-permute-start(bf16[3,16,4096]{2,1,0:T(8,128)(2,1)} %get-tuple-element.27), channel_id=1, source_target_pairs={{0,8},{1,9},{2,10},{3,11},{4,12},{5,13},{6,14},{7,15},{8,0},{9,1},... | collective-permute-start | bytes 1179656 | tf_op jit(solution)/shard_map/ppermute | solution.py:300
  51.4 93.4 %collective-permute-start.4 = (bf16[3,16,4096]{2,1,0:T(8,128)(2,1)}, bf16[3,16,4096]{2,1,0:T(8,128)(2,1)S(1)}, u32[]{:S(2)}, u32[]{:S(2)}) collective-permute-start(bf16[3,16,4096]{2,1,0:T(8,128)(2,1)} %get-tuple-element.28), channel_id=1, source_target_pairs={{0,6},{1,7},{2,8},{3,9},{4,10},{5,11},{6,12},{7,13},{8,14},{9,15},... | collective-permute-start | bytes 1179656 | tf_op jit(solution)/shard_map/ppermute | solution.py:300
  51.5 93.3 %collective-permute-start.5 = (bf16[3,16,4096]{2,1,0:T(8,128)(2,1)}, bf16[3,16,4096]{2,1,0:T(8,128)(2,1)S(1)}, u32[]{:S(2)}, u32[]{:S(2)}) collective-permute-start(bf16[3,16,4096]{2,1,0:T(8,128)(2,1)} %get-tuple-element.29), channel_id=1, source_target_pairs={{0,10},{1,11},{2,12},{3,13},{4,14},{5,15},{6,0},{7,1},{8,2},{9,3},... | collective-permute-start | bytes 1179656 | tf_op jit(solution)/shard_map/ppermute | solution.py:300
  55.9 102.8 %collective-permute-start.6 = (bf16[3,16,4096]{2,1,0:T(8,128)(2,1)}, bf16[3,16,4096]{2,1,0:T(8,128)(2,1)S(1)}, u32[]{:S(2)}, u32[]{:S(2)}) collective-permute-start(bf16[3,16,4096]{2,1,0:T(8,128)(2,1)} %get-tuple-element.30), channel_id=1, source_target_pairs={{0,4},{1,5},{2,6},{3,7},{4,8},{5,9},{6,10},{7,11},{8,12},{9,13},{1... | collective-permute-start | bytes 1179656 | tf_op jit(solution)/shard_map/ppermute | solution.py:300
  56.8 101.9 %collective-permute-start.7 = (bf16[3,16,4096]{2,1,0:T(8,128)(2,1)}, bf16[3,16,4096]{2,1,0:T(8,128)(2,1)S(1)}, u32[]{:S(2)}, u32[]{:S(2)}) collective-permute-start(bf16[3,16,4096]{2,1,0:T(8,128)(2,1)} %get-tuple-element.31), channel_id=1, source_target_pairs={{0,12},{1,13},{2,14},{3,15},{4,0},{5,1},{6,2},{7,3},{8,4},{9,5},{1... | collective-permute-start | bytes 1179656 | tf_op jit(solution)/shard_map/ppermute | solution.py:300
  93.8 0.9 copy-start.4
  94.7 9.8 %copy-start.10 = (bf16[3,16,4096]{2,1,0:T(8,128)(2,1)S(1)}, bf16[3,16,4096]{2,1,0:T(8,128)(2,1)}, u32[]{:S(2)}) copy-start(bf16[3,16,4096]{2,1,0:T(8,128)(2,1)} %copy-done.9) | copy-start | bytes 1179652
  94.7 50.1 %copy-start.8 = (bf16[3,16,4096]{2,1,0:T(8,128)(2,1)S(1)}, bf16[3,16,4096]{2,1,0:T(8,128)(2,1)}, u32[]{:S(2)}) copy-start(bf16[3,16,4096]{2,1,0:T(8,128)(2,1)} %copy-done.7) | copy-start | bytes 1179652
  104.4 60.3 %collective-permute-start.8 = (bf16[3,16,4096]{2,1,0:T(8,128)(2,1)S(1)}, bf16[3,16,4096]{2,1,0:T(8,128)(2,1)S(1)}, u32[]{:S(2)}, u32[]{:S(2)}) collective-permute-start(bf16[3,16,4096]{2,1,0:T(8,128)(2,1)S(1)} %copy-done.10), channel_id=1, source_target_pairs={{0,2},{1,3},{2,4},{3,5},{4,6},{5,7},{6,8},{7,9},{8,10},{9,11},{10,... | collective-permute-start | bytes 1179656 | tf_op jit(solution)/shard_map/ppermute | solution.py:300
  144.8 20.0 %collective-permute-start.9 = (bf16[3,16,4096]{2,1,0:T(8,128)(2,1)S(1)}, bf16[3,16,4096]{2,1,0:T(8,128)(2,1)S(1)}, u32[]{:S(2)}, u32[]{:S(2)}) collective-permute-start(bf16[3,16,4096]{2,1,0:T(8,128)(2,1)S(1)} %copy-done.8), channel_id=1, source_target_pairs={{0,14},{1,15},{2,0},{3,1},{4,2},{5,3},{6,4},{7,5},{8,6},{9,7},{10,... | collective-permute-start | bytes 1179656 | tf_op jit(solution)/shard_map/ppermute | solution.py:300

commit v4 on v3

--- a/solution.py
+++ b/solution.py
@@ -1,3 +1,4 @@
+import functools
 import math
 
 import jax
@@ -17,6 +18,8 @@
 CHIPS = 8
 ROWS = 128
 CHUNK = 2048
+SCALARS = pl.BlockSpec(memory_space=pltpu.SMEM)
+NEAR = pl.BlockSpec(memory_space=pltpu.VMEM)
 COVER = 30_000_000_000
 HELD = 6
 WIDE = 4096
@@ -170,72 +173,46 @@
     )(evens, weights)
 
 
-def gram_kernel(flags, weights_a, weights_b, *refs):
-    pieces, out, total = refs[:-2], refs[-2], refs[-1]
-    step = pl.program_id(0)
-
-    @pl.when(step == 0)
-    def _():
-        total[...] = jnp.zeros(total.shape, jnp.float32)
-
+def gram_kernel(flags, weights, *refs):
+    pieces, out = refs[:-1], refs[-1]
+    part = pieces[0].shape[-1]
     size = 2 * ROWS
-    acc = total[...]
+    sums = jnp.zeros((size, size), jnp.float32)
     for v in range(VARS):
-        spec = rows_of(pieces, v)
-        wgt_a, wgt_b = weights_a[v : v + 1, :], weights_b[v : v + 1, :]
-        wgt = jnp.concatenate([jnp.broadcast_to(wgt_a, (8, CHUNK)), jnp.broadcast_to(wgt_b, (8, CHUNK))], 0)
-        wide = spec.astype(jnp.float32).reshape(16, 16, CHUNK) * wgt[None]
-        weighted = wide.reshape(size, CHUNK).astype(jnp.bfloat16)
-        acc = acc + lax.dot_general(
-            weighted, spec, (((1,), (1,)), ((), ())), preferred_element_type=jnp.float32
-        )
-    total[...] = acc
-
-    @pl.when(step == pl.num_programs(0) - 1)
-    def _():
-        chip = flags[0] >> 1
-        sums = total[...]
-        mixed = iota((size, size), 0) ^ iota((size, size), 1)
-        same = (mixed & 14) == 0
-        signed = jnp.where((iota((size, size), 0) & 1) == 0, sums, -sums)
-        equal, other = same & ((mixed & 1) == 0), same & ((mixed & 1) == 1)
-        masked = jnp.concatenate([jnp.where(equal, sums, 0.0), jnp.where(other, signed, 0.0)], 1)
-        block, _, _, _ = row_facts((NB, size), 1, chip)
-        left = (iota((NB, size), 0) == block).astype(jnp.bfloat16)
-        block, freq, _, _ = row_facts((size, ROWS), 0, chip)
-        col = iota((size, ROWS), 1)
-        hit = (block == (col & 15)) & (freq == ((col >> 4) & 3))
-        right = jnp.concatenate([hit & (col < 64), hit & (col >= 64)], 0).astype(jnp.bfloat16)
-        gram = selected(right, selected(left, masked, True), False)
-        out[...] = jnp.broadcast_to(gram[None], out.shape)
-
-
-def piece_specs(variables, points, index):
-    even = pl.BlockSpec((CHIPS, variables, 16, points), lambda *at: (0, *index(*at)))
-    odd = pl.BlockSpec((variables, 16, points), index)
-    return [even] + [odd] * CHIPS
+        for start in range(0, part, CHUNK):
+            spec = rows_of([piece.at[..., pl.ds(start, CHUNK)] for piece in pieces], v)
+            lines = [weights[v : v + 1, pl.ds(half * part + start, CHUNK)] for half in range(2)]
+            wgt = jnp.concatenate([jnp.broadcast_to(line, (8, CHUNK)) for line in lines], 0)
+            wide = spec.astype(jnp.float32).reshape(16, 16, CHUNK) * wgt[None]
+            weighted = wide.reshape(size, CHUNK).astype(jnp.bfloat16)
+            sums = sums + lax.dot_general(
+                weighted, spec, (((1,), (1,)), ((), ())), preferred_element_type=jnp.float32
+            )
+    chip = flags[0] >> 1
+    mixed = iota((size, size), 0) ^ iota((size, size), 1)
+    same = (mixed & 14) == 0
+    signed = jnp.where((iota((size, size), 0) & 1) == 0, sums, -sums)
+    equal, other = same & ((mixed & 1) == 0), same & ((mixed & 1) == 1)
+    masked = jnp.concatenate([jnp.where(equal, sums, 0.0), jnp.where(other, signed, 0.0)], 1)
+    block, _, _, _ = row_facts((NB, size), 1, chip)
+    left = (iota((NB, size), 0) == block).astype(jnp.bfloat16)
+    block, freq, _, _ = row_facts((size, ROWS), 0, chip)
+    col = iota((size, ROWS), 1)
+    hit = (block == (col & 15)) & (freq == ((col >> 4) & 3))
+    right = jnp.concatenate([hit & (col < 64), hit & (col >= 64)], 0).astype(jnp.bfloat16)
+    gram = selected(right, selected(left, masked, True), False)
+    out[...] = jnp.broadcast_to(gram[None], out.shape)
 
 
 def gram_call(flags, pieces, weights, copies):
-    part = pieces[0].shape[-1]
-    count = part // CHUNK
     return pl.pallas_call(
         gram_kernel,
-        grid_spec=pltpu.PrefetchScalarGridSpec(
-            num_scalar_prefetch=1,
-            grid=(count,),
-            in_specs=[
-                pl.BlockSpec((VARS, CHUNK), lambda i, flags: (0, i)),
-                pl.BlockSpec((VARS, CHUNK), lambda i, flags: (0, count + i)),
-                *piece_specs(VARS, CHUNK, lambda i, flags: (0, 0, i)),
-            ],
-            out_specs=pl.BlockSpec((copies, NB, ROWS), lambda i, flags: (0, 0, 0)),
-            scratch_shapes=[pltpu.VMEM((2 * ROWS, 2 * ROWS), jnp.float32)],
-        ),
+        in_specs=[SCALARS] + [NEAR] * (1 + len(pieces)),
+        out_specs=NEAR,
         out_shape=jax.ShapeDtypeStruct((copies, NB, ROWS), jnp.float32),
         compiler_params=pltpu.CompilerParams(vmem_limit_bytes=VMEM_LIMIT),
         name="gram",
-    )(flags, weights, weights, *pieces)
+    )(flags, weights, *pieces)
 
 
 def coefficient_matrix(coef, chip):
@@ -256,40 +233,43 @@
 
 
 def modes_kernel(divisor, flags, grams, *refs):
-    pieces, out, matrix = refs[:-2], refs[-2], refs[-1]
-
-    @pl.when(pl.program_id(0) == 0)
-    def _():
-        coef = (jnp.sum(grams[...], 0) / divisor).astype(jnp.bfloat16)
-        matrix[...] = coefficient_matrix(coef, flags[0] >> 1)
-
+    pieces, out, held, sems = refs[:-3], *refs[-3:]
+    coef = (jnp.sum(grams[...], 0) / divisor).astype(jnp.bfloat16)
+    matrix = coefficient_matrix(coef, flags[0] >> 1)
     part = pieces[0].shape[-1]
-    spec = rows_of(pieces, 0)
-    for start in range(0, part, CHUNK):
-        modes = jnp.dot(
-            matrix[...], spec[:, start : start + CHUNK], preferred_element_type=jnp.float32
-        ).astype(jnp.bfloat16)
-        for half in range(2):
-            at = half * part + start
-            rows = modes[half * ROWS : (half + 1) * ROWS]
-            out[:, :, 0, :, at : at + CHUNK] = rows.reshape(OWN, NB, 2, CHUNK)
+
+    def copies(v):
+        for freq in range(OWN):
+            yield pltpu.make_async_copy(held.at[v, freq], out.at[freq, :, v], sems.at[v, freq])
+
+    for v in range(VARS):
+        spec = rows_of(pieces, v)
+        for start in range(0, part, CHUNK):
+            modes = jnp.dot(
+                matrix, spec[:, start : start + CHUNK], preferred_element_type=jnp.float32
+            ).astype(jnp.bfloat16)
+            for half in range(2):
+                at = half * part + start
+                rows = modes[half * ROWS : (half + 1) * ROWS]
+                held[v, :, :, :, at : at + CHUNK] = rows.reshape(OWN, NB, 2, CHUNK)
+        for copy in copies(v):
+            copy.start()
+    for v in range(VARS):
+        for copy in copies(v):
+            copy.wait()
 
 
 def modes_call(flags, grams, pieces, divisor):
-    part = pieces[0].shape[-1]
-    return pl.pallas_call(
-        lambda *refs: modes_kernel(divisor, *refs),
-        grid_spec=pltpu.PrefetchScalarGridSpec(
-            num_scalar_prefetch=1,
-            grid=(VARS,),
-            in_specs=[
-                pl.BlockSpec(grams.shape, lambda v, flags: (0, 0, 0)),
-                *piece_specs(1, part, lambda v, flags: (v, 0, 0)),
-            ],
-            out_specs=pl.BlockSpec((OWN, NB, 1, 2, 2 * part), lambda v, flags: (0, 0, v, 0, 0)),
-            scratch_shapes=[pltpu.VMEM((2 * ROWS, 2 * ROWS), jnp.bfloat16)],
-        ),
-        out_shape=jax.ShapeDtypeStruct((OWN, NB, VARS, 2, 2 * part), jnp.bfloat16),
+    points = 2 * pieces[0].shape[-1]
+    return pl.pallas_call(
+        functools.partial(modes_kernel, divisor),
+        in_specs=[SCALARS] + [NEAR] * (1 + len(pieces)),
+        out_specs=pl.BlockSpec(memory_space=pl.ANY),
+        scratch_shapes=[
+            pltpu.VMEM((VARS, OWN, NB, 2, points), jnp.bfloat16),
+            pltpu.SemaphoreType.DMA((VARS, OWN)),
+        ],
+        out_shape=jax.ShapeDtypeStruct((OWN, NB, VARS, 2, points), jnp.bfloat16),
         compiler_params=pltpu.CompilerParams(vmem_limit_bytes=VMEM_LIMIT),
         name="modes",
     )(flags, grams, *pieces)
@@ -311,7 +291,6 @@
     own = lax.dynamic_slice_in_dim(record, (index & 1) * part, part, 2)
     before = [(2 * z + 2, 2 * z) for z in range(CHIPS - 1)]
     after = [((2 * z - 1) % NB, 2 * z + 1) for z in range(CHIPS)]
-    own, record = lax.optimization_barrier((own, record))
     halo = lax.ppermute(own, "tm", before + after)
     beside = lax.ppermute(record, "tm", across)
     evens = dft_even(flags, record, beside)

time: 187 us -> 185 us (0.989)
  waiting for transfers between devices: 97.2 us -> 109 us
  starting transfers between devices: 42.5 us -> 32.8 us
  local copies, waits for them, and re-layouts: 14.2 us -> 10.4 us
    all_to_all x1, waiting for transfers between devices: 34.3 us -> 47.7 us  [shards(): lax.all_to_all(evens, 'tm', split_axis=0, concat_axis=0, axis_index_group...]
    ppermute x1, waiting for transfers between devices: 8.65 us -> 19.5 us  [shards(): halo = lax.ppermute(own, 'tm', before + after)]
    ppermute x7, waiting for transfers between devices: 47.3 us -> 37 us  [shifted_by(): return lax.ppermute(value, 'tm', pairs)]
    ppermute x7, starting transfers between devices: 30.9 us -> 21 us  [shifted_by(): return lax.ppermute(value, 'tm', pairs)]
    unnamed x24 -> x20, local copies, waits for them, and re-layouts: 11.3 us -> 7.65 us
    ppermute x1, waiting for transfers between devices: 3.37 us -> 0.76 us  [shards(): beside = lax.ppermute(record, 'tm', across)]
  transfers between devices with their start and end apart: 11 -> 11, of which waited for: 8 -> 8; matrix products, arithmetic and copies ran while one was open for 0% -> 2% of each run, Pallas kernels for 6% -> 7%
where the time goes in v4:
time: 185 us
  waiting for transfers between devices  109 us (59%)
  starting transfers between devices  32.8 us (18%)
  Pallas kernels  19.6 us (11%)
  blocking collectives  13.3 us (7%)
  local copies, waits for them, and re-layouts  10.4 us (6%)
    all_to_all x1, waiting for transfers between devices, shards(): lax.all_to_all(evens, 'tm', split_axis=0, concat_axis=0, axis_index_group...  47.7 us
    ppermute x7, waiting for transfers between devices, shifted_by(): return lax.ppermute(value, 'tm', pairs)  37 us
    ppermute x7, starting transfers between devices, shifted_by(): return lax.ppermute(value, 'tm', pairs)  21 us
    ppermute x1, waiting for transfers between devices, shards(): halo = lax.ppermute(own, 'tm', before + after)  19.5 us
    all_to_all x1, blocking collectives, shards(): lax.all_to_all(grams, 'pts', split_axis=0, concat_axis=0, tiled=True)  13.3 us
    unnamed x20, local copies, waits for them, and re-layouts  7.65 us
    all_to_all x1, starting transfers between devices, shards(): lax.all_to_all(evens, 'tm', split_axis=0, concat_axis=0, axis_index_group...  6.56 us
    pallas_call x1, Pallas kernels, dft_odd(): pl.pallas_call(dft_odd_kernel, grid_spec=pltpu.PrefetchScalarGridSpec(num...  4.94 us
  transfers between devices with their start and end apart: 11, of which 8 were waited for; matrix products, arithmetic and copies ran while one was open for 2% of the time, Pallas kernels for 7%

profile of v4, /device:TPU:1, one launch (start us, length us, event | category | flops | bytes accessed | tf_op | source)
XLA Modules:
  0.0 184.8 jit_solution(5821994449992922851)
XLA Ops:
  0.0 3.2 %collective-permute-start = (bf16[3,64,8192]{2,1,0:T(8,128)(2,1)}, bf16[3,64,8192]{2,1,0:T(8,128)(2,1)}, u32[]{:S(2)}, u32[]{:S(2)}) collective-permute-start(bf16[3,64,8192]{2,1,0:T(8,128)(2,1)} %bitcast.6), channel_id=1, source_target_pairs={{0,1},{1,0},{2,3},{3,2},{4,5},{5,4},{6,7},{7,6},{8,9},{9,8},{10,11... | collective-permute-start | bytes 9437192 | tf_op jit(solution)/shard_map/ppermute | solution.py:295
  3.2 2.8 %dynamic-slice_bitcast_fusion = bf16[3,64,4096]{2,1,0:T(8,128)(2,1)} fusion(bf16[64,3,8192]{2,0,1:T(8,128)(2,1)} %param.5, s32[]{:T(128)S(6)} %select_n.3), kind=kLoop, calls=%fused_computation | loop fusion | bytes 3145732 | tf_op jit(solution)/shard_map/dynamic_slice | solution.py:291
  6.0 2.1 %collective-permute-start.1 = (bf16[3,64,4096]{2,1,0:T(8,128)(2,1)}, bf16[3,64,4096]{2,1,0:T(8,128)(2,1)}, u32[]{:S(2)}, u32[]{:S(2)}) collective-permute-start(bf16[3,64,4096]{2,1,0:T(8,128)(2,1)} %dynamic-slice_bitcast_fusion), channel_id=1, source_target_pairs={{2,0},{4,2},{6,4},{8,6},{10,8},{12,10},{14,12},{15,1},{1,3},{3,5},... | collective-permute-start | bytes 4718600 | tf_op jit(solution)/shard_map/ppermute | solution.py:294
  9.6 3.6 %dft_even.1 = bf16[8,3,16,4096]{3,2,1,0:T(8,128)(2,1)S(1)} custom-call(s32[1]{0:T(128)} %bitcast.flags, bf16[2,64,128]{2,1,0:T(8,128)(2,1)S(1)} %copy-done.3, bf16[3,64,8192]{2,1,0:T(8,128)(2,1)S(1)} %bitcast.7, bf16[3,64,8192]{2,1,0:T(8,128)(2,1)S(1)} %bitcast.8, bf16[3,64,8192]{2,1,0:T(8,128)(2,1)} %collective-permute-done.beside_a.beside_b, ...), custom_call_target="tpu_custom_call" | custom-call | tf_op jit(solution)/shard_map/dft_even/pallas_call | solution.py:75
  13.2 1.7 copy-done.1
  14.9 6.6 %all-to-all-start = ((bf16[8,3,16,4096]{3,2,1,0:T(8,128)(2,1)}), bf16[8,3,16,4096]{3,2,1,0:T(8,128)(2,1)}, u32[]{:S(2)}, u32[]{:S(2)}) async-start(bf16[8,3,16,4096]{3,2,1,0:T(8,128)(2,1)} %copy-done.1), calls=%async_computation | async-start | bytes 6291456 | tf_op jit(solution)/shard_map/all_to_all | solution.py:298
  21.4 19.5 %collective-permute-done.1.halo = bf16[3,64,4096]{2,1,0:T(8,128)(2,1)} collective-permute-done((bf16[3,64,4096]{2,1,0:T(8,128)(2,1)}, bf16[3,64,4096]{2,1,0:T(8,128)(2,1)}, u32[]{:S(2)}, u32[]{:S(2)}) %collective-permute-start.1) | collective-permute-done | bytes 1572896 | tf_op jit(solution)/shard_map/ppermute | solution.py:294
  41.0 3.6 %collective-permute-done.2.swapped = bf16[3,64,4096]{2,1,0:T(8,128)(2,1)S(1)} collective-permute-done((bf16[3,64,4096]{2,1,0:T(8,128)(2,1)}, bf16[3,64,4096]{2,1,0:T(8,128)(2,1)S(1)}, u32[]{:S(2)}, u32[]{:S(2)}) %collective-permute-start.2) | collective-permute-done | bytes 1572896 | tf_op jit(solution)/shard_map/ppermute | solution.py:299
  44.6 1.9 %copy-done.4 = bf16[64,3,8192]{2,0,1:T(8,128)(2,1)S(1)} copy-done((bf16[64,3,8192]{2,0,1:T(8,128)(2,1)S(1)}, bf16[64,3,8192]{2,0,1:T(8,128)(2,1)}, u32[]{:S(2)}) %copy-start.4) | copy-done | bytes 3145752
  46.5 0.9 copy-done.9
  47.4 4.9 %dft_odd.1 = (bf16[3,16,4096]{2,1,0:T(8,128)(2,1)}, bf16[3,16,4096]{2,1,0:T(8,128)(2,1)}, bf16[3,16,4096]{2,1,0:T(8,128)(2,1)}, bf16[3,16,4096]{2,1,0:T(8,128)(2...) custom-call(s32[1]{0:T(128)} %bitcast.flags, ...), custom_call_target="tpu_custom_call" | custom-call | flops 30000001024 | bytes 30000001024 | tf_op jit(solution)/shard_map/dft_odd/pallas_call | solution.py:122
  53.8 7.3 %collective-permute-start.3 = (bf16[3,16,4096]{2,1,0:T(8,128)(2,1)}, bf16[3,16,4096]{2,1,0:T(8,128)(2,1)S(1)}, u32[]{:S(2)}, u32[]{:S(2)}) collective-permute-start(bf16[3,16,4096]{2,1,0:T(8,128)(2,1)} %get-tuple-element.23), channel_id=1, source_target_pairs={{0,8},{1,9},{2,10},{3,11},{4,12},{5,13},{6,14},{7,15},{8,0},{9,1},... | collective-permute-start | bytes 1179656 | tf_op jit(solution)/shard_map/ppermute | solution.py:280
  61.2 4.5 %collective-permute-start.5 = (bf16[3,16,4096]{2,1,0:T(8,128)(2,1)}, bf16[3,16,4096]{2,1,0:T(8,128)(2,1)S(1)}, u32[]{:S(2)}, u32[]{:S(2)}) collective-permute-start(bf16[3,16,4096]{2,1,0:T(8,128)(2,1)} %get-tuple-element.25), channel_id=1, source_target_pairs={{0,10},{1,11},{2,12},{3,13},{4,14},{5,15},{6,0},{7,1},{8,2},{9,3},... | collective-permute-start | bytes 1179656 | tf_op jit(solution)/shard_map/ppermute | solution.py:280
  66.6 2.7 %collective-permute-start.7 = (bf16[3,16,4096]{2,1,0:T(8,128)(2,1)}, bf16[3,16,4096]{2,1,0:T(8,128)(2,1)S(1)}, u32[]{:S(2)}, u32[]{:S(2)}) collective-permute-start(bf16[3,16,4096]{2,1,0:T(8,128)(2,1)} %get-tuple-element.27), channel_id=1, source_target_pairs={{0,12},{1,13},{2,14},{3,15},{4,0},{5,1},{6,2},{7,3},{8,4},{9,5},{1... | collective-permute-start | bytes 1179656 | tf_op jit(solution)/shard_map/ppermute | solution.py:280
  69.2 47.7 %all-to-all-done.evens = bf16[8,3,16,4096]{3,2,1,0:T(8,128)(2,1)} async-done(((bf16[8,3,16,4096]{3,2,1,0:T(8,128)(2,1)}), bf16[8,3,16,4096]{3,2,1,0:T(8,128)(2,1)}, u32[]{:S(2)}, u32[]{:S(2)}) %all-to-all-start) | async-done | bytes 3145760 | tf_op jit(solution)/shard_map/all_to_all | solution.py:298
  117.8 4.4 %held.1 = (bf16[8,3,16,4096]{3,2,1,0:T(8,128)(2,1)S(1)}, f32[3,8192]{1,0:T(4,128)S(1)}) custom-call(bf16[8,3,16,4096]{3,2,1,0:T(8,128)(2,1)} %all-to-all-done.evens, f32[3,8192]{1,0:T(4,128)S(1)} %copy-done.2), custom_call_target="tpu_custom_call" | custom-call | tf_op jit(solution)/shard_map/held/pallas_call | solution.py:162
  122.3 1.5 collective-permute-done.3.refs_1_
  123.8 5.6 %collective-permute-start.8 = (bf16[3,16,4096]{2,1,0:T(8,128)(2,1)S(1)}, bf16[3,16,4096]{2,1,0:T(8,128)(2,1)S(1)}, u32[]{:S(2)}, u32[]{:S(2)}) collective-permute-start(bf16[3,16,4096]{2,1,0:T(8,128)(2,1)S(1)} %copy-done.8), channel_id=1, source_target_pairs={{0,2},{1,3},{2,4},{3,5},{4,6},{5,7},{6,8},{7,9},{8,10},{9,11},{10,... | collective-permute-start | bytes 1179656 | tf_op jit(solution)/shard_map/ppermute | solution.py:280
  129.3 19.1 %collective-permute-done.4.refs_2_ = bf16[3,16,4096]{2,1,0:T(8,128)(2,1)S(1)} collective-permute-done((bf16[3,16,4096]{2,1,0:T(8,128)(2,1)}, bf16[3,16,4096]{2,1,0:T(8,128)(2,1)S(1)}, u32[]{:S(2)}, u32[]{:S(2)}) %collective-permute-start.4) | collective-permute-done | bytes 393248 | tf_op jit(solution)/shard_map/ppermute | solution.py:280
  148.5 13.2 %collective-permute-done.6.refs_4_ = bf16[3,16,4096]{2,1,0:T(8,128)(2,1)S(1)} collective-permute-done((bf16[3,16,4096]{2,1,0:T(8,128)(2,1)}, bf16[3,16,4096]{2,1,0:T(8,128)(2,1)S(1)}, u32[]{:S(2)}, u32[]{:S(2)}) %collective-permute-start.6) | collective-permute-done | bytes 393248 | tf_op jit(solution)/shard_map/ppermute | solution.py:280
  161.6 3.3 %collective-permute-done.8.refs_6_ = bf16[3,16,4096]{2,1,0:T(8,128)(2,1)S(1)} collective-permute-done((bf16[3,16,4096]{2,1,0:T(8,128)(2,1)S(1)}, bf16[3,16,4096]{2,1,0:T(8,128)(2,1)S(1)}, u32[]{:S(2)}, u32[]{:S(2)}) %collective-permute-start.8) | collective-permute-done | bytes 393248 | tf_op jit(solution)/shard_map/ppermute | solution.py:280
  164.9 2.6 %gram.1 = f32[16,16,128]{2,1,0:T(8,128)S(1)} custom-call(s32[1]{0:T(128)} %bitcast.flags, f32[3,8192]{1,0:T(4,128)S(1)} %get-tuple-element.21.weights, bf16[8,3,16,4096]{3,2,1,0:T(8,128)(2,1)S(1)} %get-tuple-element.22.refs_0_, bf16[3,16,4096]{2,1,0:T(8,128)(2,1)S(1)} %collective-permute-done.3.refs_1_, ...), custom_call_target="tpu_custom_call" | custom-call | tf_op jit(solution)/shard_map/gram/pallas_call | solution.py:208
  167.5 13.3 %all_to_all.10.grams = f32[16,16,128]{2,1,0:T(8,128)S(1)} all-to-all(f32[16,16,128]{2,1,0:T(8,128)S(1)} %gram.1), channel_id=1, replica_groups=mesh['pts'=16,'tm'=16] {'pts'}, dimensions={0} | all-to-all | bytes 262144 | tf_op jit(solution)/shard_map/all_to_all | solution.py:307
  180.8 4.0 %modes.1 = bf16[4,16,3,2,8192]{4,3,2,1,0:T(2,128)(2,1)} custom-call(s32[1]{0:T(128)} %bitcast.flags, f32[16,16,128]{2,1,0:T(8,128)S(1)} %all_to_all.10.grams, bf16[8,3,16,4096]{3,2,1,0:T(8,128)(2,1)S(1)} %get-tuple-element.22.refs_0_, bf16[3,16,4096]{2,1,0:T(8,128)(2,1)S(1)} %collective-permute-done.3.refs_1_, ...), custom_call_target="tpu_custom_call" | custom-call | tf_op jit(solution)/shard_map/modes/pallas_call | solution.py:264
  (25 shorter events, 4.8 us)
Async XLA Ops:
  0.0 8.9 %copy-start = (bf16[64,3,8192]{2,0,1:T(8,128)(2,1)S(1)}, bf16[64,3,8192]{2,0,1:T(8,128)(2,1)}, u32[]{:S(2)}) copy-start(bf16[64,3,8192]{2,0,1:T(8,128)(2,1)} %param.5) | copy-start | bytes 9437188
  0.0 8.9 %collective-permute-start = (bf16[3,64,8192]{2,1,0:T(8,128)(2,1)}, bf16[3,64,8192]{2,1,0:T(8,128)(2,1)}, u32[]{:S(2)}, u32[]{:S(2)}) collective-permute-start(bf16[3,64,8192]{2,1,0:T(8,128)(2,1)} %bitcast.6), channel_id=1, source_target_pairs={{0,1},{1,0},{2,3},{3,2},{4,5},{5,4},{6,7},{7,6},{8,9},{9,8},{10,11... | collective-permute-start | bytes 9437192 | tf_op jit(solution)/shard_map/ppermute | solution.py:295
  6.0 34.9 %collective-permute-start.1 = (bf16[3,64,4096]{2,1,0:T(8,128)(2,1)}, bf16[3,64,4096]{2,1,0:T(8,128)(2,1)}, u32[]{:S(2)}, u32[]{:S(2)}) collective-permute-start(bf16[3,64,4096]{2,1,0:T(8,128)(2,1)} %dynamic-slice_bitcast_fusion), channel_id=1, source_target_pairs={{2,0},{4,2},{6,4},{8,6},{10,8},{12,10},{14,12},{15,1},{1,3},{3,5},... | collective-permute-start | bytes 4718600 | tf_op jit(solution)/shard_map/ppermute | solution.py:294
  8.9 0.8 copy-start.3
  13.2 1.7 copy-start.1
  14.9 102.1 %all-to-all-start = ((bf16[8,3,16,4096]{3,2,1,0:T(8,128)(2,1)}), bf16[8,3,16,4096]{3,2,1,0:T(8,128)(2,1)}, u32[]{:S(2)}, u32[]{:S(2)}) async-start(bf16[8,3,16,4096]{3,2,1,0:T(8,128)(2,1)} %copy-done.1), calls=%async_computation | async-start | bytes 6291456 | tf_op jit(solution)/shard_map/all_to_all | solution.py:298
  41.0 3.6 %collective-permute-start.2 = (bf16[3,64,4096]{2,1,0:T(8,128)(2,1)}, bf16[3,64,4096]{2,1,0:T(8,128)(2,1)S(1)}, u32[]{:S(2)}, u32[]{:S(2)}) collective-permute-start(bf16[3,64,4096]{2,1,0:T(8,128)(2,1)} %collective-permute-done.1.halo), channel_id=1, source_target_pairs={{0,1},{1,0},{2,3},{3,2},{4,5},{5,4},{6,7},{7,6},{8,9},{9,8},{10,11... | collective-permute-start | bytes 4718600 | tf_op jit(solution)/shard_map/ppermute | solution.py:299
  44.6 1.9 %copy-start.4 = (bf16[64,3,8192]{2,0,1:T(8,128)(2,1)S(1)}, bf16[64,3,8192]{2,0,1:T(8,128)(2,1)}, u32[]{:S(2)}) copy-start(bf16[64,3,8192]{2,0,1:T(8,128)(2,1)} %param.6) | copy-start | bytes 9437188
  46.5 0.9 copy-start.9
  52.4 0.7 copy-start.5
  53.1 0.7 copy-start.7
  53.8 69.9 %collective-permute-start.3 = (bf16[3,16,4096]{2,1,0:T(8,128)(2,1)}, bf16[3,16,4096]{2,1,0:T(8,128)(2,1)S(1)}, u32[]{:S(2)}, u32[]{:S(2)}) collective-permute-start(bf16[3,16,4096]{2,1,0:T(8,128)(2,1)} %get-tuple-element.23), channel_id=1, source_target_pairs={{0,8},{1,9},{2,10},{3,11},{4,12},{5,13},{6,14},{7,15},{8,0},{9,1},... | collective-permute-start | bytes 1179656 | tf_op jit(solution)/shard_map/ppermute | solution.py:280
  61.2 87.3 %collective-permute-start.4 = (bf16[3,16,4096]{2,1,0:T(8,128)(2,1)}, bf16[3,16,4096]{2,1,0:T(8,128)(2,1)S(1)}, u32[]{:S(2)}, u32[]{:S(2)}) collective-permute-start(bf16[3,16,4096]{2,1,0:T(8,128)(2,1)} %get-tuple-element.24), channel_id=1, source_target_pairs={{0,6},{1,7},{2,8},{3,9},{4,10},{5,11},{6,12},{7,13},{8,14},{9,15},... | collective-permute-start | bytes 1179656 | tf_op jit(solution)/shard_map/ppermute | solution.py:280
  61.2 87.3 %collective-permute-start.5 = (bf16[3,16,4096]{2,1,0:T(8,128)(2,1)}, bf16[3,16,4096]{2,1,0:T(8,128)(2,1)S(1)}, u32[]{:S(2)}, u32[]{:S(2)}) collective-permute-start(bf16[3,16,4096]{2,1,0:T(8,128)(2,1)} %get-tuple-element.25), channel_id=1, source_target_pairs={{0,10},{1,11},{2,12},{3,13},{4,14},{5,15},{6,0},{7,1},{8,2},{9,3},... | collective-permute-start | bytes 1179656 | tf_op jit(solution)/shard_map/ppermute | solution.py:280
  65.7 96.0 %collective-permute-start.6 = (bf16[3,16,4096]{2,1,0:T(8,128)(2,1)}, bf16[3,16,4096]{2,1,0:T(8,128)(2,1)S(1)}, u32[]{:S(2)}, u32[]{:S(2)}) collective-permute-start(bf16[3,16,4096]{2,1,0:T(8,128)(2,1)} %get-tuple-element.26), channel_id=1, source_target_pairs={{0,4},{1,5},{2,6},{3,7},{4,8},{5,9},{6,10},{7,11},{8,12},{9,13},{1... | collective-permute-start | bytes 1179656 | tf_op jit(solution)/shard_map/ppermute | solution.py:280
  66.6 95.1 %collective-permute-start.7 = (bf16[3,16,4096]{2,1,0:T(8,128)(2,1)}, bf16[3,16,4096]{2,1,0:T(8,128)(2,1)S(1)}, u32[]{:S(2)}, u32[]{:S(2)}) collective-permute-start(bf16[3,16,4096]{2,1,0:T(8,128)(2,1)} %get-tuple-element.27), channel_id=1, source_target_pairs={{0,12},{1,13},{2,14},{3,15},{4,0},{5,1},{6,2},{7,3},{8,4},{9,5},{1... | collective-permute-start | bytes 1179656 | tf_op jit(solution)/shard_map/ppermute | solution.py:280
  116.9 0.9 copy-start.2
  117.8 5.9 %copy-start.8 = (bf16[3,16,4096]{2,1,0:T(8,128)(2,1)S(1)}, bf16[3,16,4096]{2,1,0:T(8,128)(2,1)}, u32[]{:S(2)}) copy-start(bf16[3,16,4096]{2,1,0:T(8,128)(2,1)} %copy-done.7) | copy-start | bytes 1179652
  117.8 30.6 %copy-start.6 = (bf16[3,16,4096]{2,1,0:T(8,128)(2,1)S(1)}, bf16[3,16,4096]{2,1,0:T(8,128)(2,1)}, u32[]{:S(2)}) copy-start(bf16[3,16,4096]{2,1,0:T(8,128)(2,1)} %copy-done.5) | copy-start | bytes 1179652
  123.8 41.1 %collective-permute-start.8 = (bf16[3,16,4096]{2,1,0:T(8,128)(2,1)S(1)}, bf16[3,16,4096]{2,1,0:T(8,128)(2,1)S(1)}, u32[]{:S(2)}, u32[]{:S(2)}) collective-permute-start(bf16[3,16,4096]{2,1,0:T(8,128)(2,1)S(1)} %copy-done.8), channel_id=1, source_target_pairs={{0,2},{1,3},{2,4},{3,5},{4,6},{5,7},{6,8},{7,9},{8,10},{9,11},{10,... | collective-permute-start | bytes 1179656 | tf_op jit(solution)/shard_map/ppermute | solution.py:280
  148.5 16.4 %collective-permute-start.9 = (bf16[3,16,4096]{2,1,0:T(8,128)(2,1)S(1)}, bf16[3,16,4096]{2,1,0:T(8,128)(2,1)S(1)}, u32[]{:S(2)}, u32[]{:S(2)}) collective-permute-start(bf16[3,16,4096]{2,1,0:T(8,128)(2,1)S(1)} %copy-done.6), channel_id=1, source_target_pairs={{0,14},{1,15},{2,0},{3,1},{4,2},{5,3},{6,4},{7,5},{8,6},{9,7},{10,... | collective-permute-start | bytes 1179656 | tf_op jit(solution)/shard_map/ppermute | solution.py:280

commit v5 on v4

--- a/solution.py
+++ b/solution.py
@@ -23,7 +23,7 @@
 COVER = 30_000_000_000
 HELD = 6
 WIDE = 4096
-VMEM_LIMIT = 28 * 1024 * 1024
+VMEM_LIMIT = 20 * 1024 * 1024
 SHIFTS = (4, 3, 5, 2, 6, 1, 7, 0)
 
 
@@ -150,30 +150,43 @@
     return jnp.concatenate([evens, *(piece[v] for piece in pieces[1:])], 0)
 
 
-def held_kernel(evens, weights, evens_out, weights_out):
+def held_kernel(flags, evens, weights, evens_out, weights_out, left, right):
     evens_out[...] = evens[...]
     weights_out[...] = weights[...]
 
-
-def held_call(evens, weights):
+    @pl.when(pl.program_id(0) == 0)
+    def _():
+        chip, size = flags[0] >> 1, 2 * ROWS
+        block, _, _, _ = row_facts((NB, size), 1, chip)
+        left[...] = (iota((NB, size), 0) == block).astype(jnp.bfloat16)
+        block, freq, _, _ = row_facts((size, ROWS), 0, chip)
+        col = iota((size, ROWS), 1)
+        hit = (block == (col & 15)) & (freq == ((col >> 4) & 3))
+        right[...] = jnp.concatenate([hit & (col < 64), hit & (col >= 64)], 0).astype(jnp.bfloat16)
+
+
+def held_call(flags, evens, weights):
     part = evens.shape[-1]
     piece = pl.BlockSpec((1, VARS, 16, part), lambda i: (i, 0, 0, 0))
-    line = pl.BlockSpec(weights.shape, lambda i: (0, 0))
+    whole = lambda shape: pl.BlockSpec(shape, lambda i: (0, 0))
+    left, right = (NB, 2 * ROWS), (4 * ROWS, ROWS)
     return pl.pallas_call(
         held_kernel,
         grid=(CHIPS,),
-        in_specs=[piece, line],
-        out_specs=[piece, line],
+        in_specs=[SCALARS, piece, whole(weights.shape)],
+        out_specs=[piece, whole(weights.shape), whole(left), whole(right)],
         out_shape=[
             jax.ShapeDtypeStruct(evens.shape, evens.dtype),
             jax.ShapeDtypeStruct(weights.shape, weights.dtype),
+            jax.ShapeDtypeStruct(left, jnp.bfloat16),
+            jax.ShapeDtypeStruct(right, jnp.bfloat16),
         ],
         compiler_params=pltpu.CompilerParams(vmem_limit_bytes=VMEM_LIMIT),
         name="held",
-    )(evens, weights)
-
-
-def gram_kernel(flags, weights, *refs):
+    )(flags, evens, weights)
+
+
+def gram_kernel(left, right, weights, *refs):
     pieces, out = refs[:-1], refs[-1]
     part = pieces[0].shape[-1]
     size = 2 * ROWS
@@ -188,31 +201,24 @@
             sums = sums + lax.dot_general(
                 weighted, spec, (((1,), (1,)), ((), ())), preferred_element_type=jnp.float32
             )
-    chip = flags[0] >> 1
     mixed = iota((size, size), 0) ^ iota((size, size), 1)
     same = (mixed & 14) == 0
     signed = jnp.where((iota((size, size), 0) & 1) == 0, sums, -sums)
     equal, other = same & ((mixed & 1) == 0), same & ((mixed & 1) == 1)
     masked = jnp.concatenate([jnp.where(equal, sums, 0.0), jnp.where(other, signed, 0.0)], 1)
-    block, _, _, _ = row_facts((NB, size), 1, chip)
-    left = (iota((NB, size), 0) == block).astype(jnp.bfloat16)
-    block, freq, _, _ = row_facts((size, ROWS), 0, chip)
-    col = iota((size, ROWS), 1)
-    hit = (block == (col & 15)) & (freq == ((col >> 4) & 3))
-    right = jnp.concatenate([hit & (col < 64), hit & (col >= 64)], 0).astype(jnp.bfloat16)
-    gram = selected(right, selected(left, masked, True), False)
+    gram = selected(right[...], selected(left[...], masked, True), False)
     out[...] = jnp.broadcast_to(gram[None], out.shape)
 
 
-def gram_call(flags, pieces, weights, copies):
+def gram_call(selections, pieces, weights, copies):
     return pl.pallas_call(
         gram_kernel,
-        in_specs=[SCALARS] + [NEAR] * (1 + len(pieces)),
+        in_specs=[NEAR] * (3 + len(pieces)),
         out_specs=NEAR,
         out_shape=jax.ShapeDtypeStruct((copies, NB, ROWS), jnp.float32),
         compiler_params=pltpu.CompilerParams(vmem_limit_bytes=VMEM_LIMIT),
         name="gram",
-    )(flags, weights, *pieces)
+    )(*selections, weights, *pieces)
 
 
 def coefficient_matrix(coef, chip):
@@ -298,12 +304,12 @@
     evens = lax.all_to_all(evens, "tm", split_axis=0, concat_axis=0, axis_index_groups=groups, tiled=True)
     swapped = lax.ppermute(halo, "tm", across)
     odds = [*dft_odd(flags, record, beside, halo, swapped, tail)]
-    evens, quad_weights = held_call(evens, quad_weights)
+    evens, quad_weights, *selections = held_call(flags, evens, quad_weights)
     evens, quad_weights, odds[HELD] = lax.optimization_barrier((evens, quad_weights, odds[HELD]))
     odds = [shifted_by(odd, shift) if shift else odd for odd, shift in zip(odds, SHIFTS)]
     pieces = [evens, *odds]
     slabs = lax.axis_size("pts")
-    grams = gram_call(flags, pieces, quad_weights, slabs)
+    grams = gram_call(selections, pieces, quad_weights, slabs)
     grams = lax.all_to_all(grams, "pts", split_axis=0, concat_axis=0, tiled=True)
     modes = modes_call(flags, grams, pieces, float(VARS * points * slabs))
     return jnp.transpose(modes, (0, 1, 3, 2, 4))

time: 185 us -> 185 us (level)
  no operation moved by 1% of the time
where the time goes in v5:
time: 185 us
  waiting for transfers between devices  108 us (58%)
  starting transfers between devices  33 us (18%)
  Pallas kernels  19.7 us (11%)
  blocking collectives  13.3 us (7%)
  local copies, waits for them, and re-layouts  10.4 us (6%)
    all_to_all x1, waiting for transfers between devices, shards(): lax.all_to_all(evens, 'tm', split_axis=0, concat_axis=0, axis_index_group...  47.7 us
    ppermute x7, waiting for transfers between devices, shifted_by(): return lax.ppermute(value, 'tm', pairs)  36.6 us
    ppermute x7, starting transfers between devices, shifted_by(): return lax.ppermute(value, 'tm', pairs)  21.2 us
    ppermute x1, waiting for transfers between devices, shards(): halo = lax.ppermute(own, 'tm', before + after)  19.5 us
    all_to_all x1, blocking collectives, shards(): lax.all_to_all(grams, 'pts', split_axis=0, concat_axis=0, tiled=True)  13.3 us
    unnamed x20, local copies, waits for them, and re-layouts  7.65 us
    all_to_all x1, starting transfers between devices, shards(): lax.all_to_all(evens, 'tm', split_axis=0, concat_axis=0, axis_index_group...  6.56 us
    pallas_call x1, Pallas kernels, dft_odd(): pl.pallas_call(dft_odd_kernel, grid_spec=pltpu.PrefetchScalarGridSpec(num...  4.94 us
  transfers between devices with their start and end apart: 11, of which 8 were waited for; matrix products, arithmetic and copies ran while one was open for 2% of the time, Pallas kernels for 7%

profile of v5, /device:TPU:1, one launch (start us, length us, event | category | flops | bytes accessed | tf_op | source)
XLA Modules:
  0.0 184.7 jit_solution(9104205704282816948)
XLA Ops:
  0.0 3.2 %collective-permute-start = (bf16[3,64,8192]{2,1,0:T(8,128)(2,1)}, bf16[3,64,8192]{2,1,0:T(8,128)(2,1)}, u32[]{:S(2)}, u32[]{:S(2)}) collective-permute-start(bf16[3,64,8192]{2,1,0:T(8,128)(2,1)} %bitcast.6), channel_id=1, source_target_pairs={{0,1},{1,0},{2,3},{3,2},{4,5},{5,4},{6,7},{7,6},{8,9},{9,8},{10,11... | collective-permute-start | bytes 9437192 | tf_op jit(solution)/shard_map/ppermute | solution.py:301
  3.2 2.8 %dynamic-slice_bitcast_fusion = bf16[3,64,4096]{2,1,0:T(8,128)(2,1)} fusion(bf16[64,3,8192]{2,0,1:T(8,128)(2,1)} %param.5, s32[]{:T(128)S(6)} %select_n.3), kind=kLoop, calls=%fused_computation | loop fusion | bytes 3145732 | tf_op jit(solution)/shard_map/dynamic_slice | solution.py:297
  6.0 2.1 %collective-permute-start.1 = (bf16[3,64,4096]{2,1,0:T(8,128)(2,1)}, bf16[3,64,4096]{2,1,0:T(8,128)(2,1)}, u32[]{:S(2)}, u32[]{:S(2)}) collective-permute-start(bf16[3,64,4096]{2,1,0:T(8,128)(2,1)} %dynamic-slice_bitcast_fusion), channel_id=1, source_target_pairs={{2,0},{4,2},{6,4},{8,6},{10,8},{12,10},{14,12},{15,1},{1,3},{3,5},... | collective-permute-start | bytes 4718600 | tf_op jit(solution)/shard_map/ppermute | solution.py:300
  9.6 3.6 %dft_even.1 = bf16[8,3,16,4096]{3,2,1,0:T(8,128)(2,1)S(1)} custom-call(s32[1]{0:T(128)} %bitcast.flags, bf16[2,64,128]{2,1,0:T(8,128)(2,1)S(1)} %copy-done.3, bf16[3,64,8192]{2,1,0:T(8,128)(2,1)S(1)} %bitcast.7, bf16[3,64,8192]{2,1,0:T(8,128)(2,1)S(1)} %bitcast.8, bf16[3,64,8192]{2,1,0:T(8,128)(2,1)} %collective-permute-done.beside_a.beside_b, ...), custom_call_target="tpu_custom_call" | custom-call | tf_op jit(solution)/shard_map/dft_even/pallas_call | solution.py:75
  13.2 1.7 copy-done.1
  14.9 6.6 %all-to-all-start = ((bf16[8,3,16,4096]{3,2,1,0:T(8,128)(2,1)}), bf16[8,3,16,4096]{3,2,1,0:T(8,128)(2,1)}, u32[]{:S(2)}, u32[]{:S(2)}) async-start(bf16[8,3,16,4096]{3,2,1,0:T(8,128)(2,1)} %copy-done.1), calls=%async_computation | async-start | bytes 6291456 | tf_op jit(solution)/shard_map/all_to_all | solution.py:304
  21.4 19.5 %collective-permute-done.1.halo = bf16[3,64,4096]{2,1,0:T(8,128)(2,1)} collective-permute-done((bf16[3,64,4096]{2,1,0:T(8,128)(2,1)}, bf16[3,64,4096]{2,1,0:T(8,128)(2,1)}, u32[]{:S(2)}, u32[]{:S(2)}) %collective-permute-start.1) | collective-permute-done | bytes 1572896 | tf_op jit(solution)/shard_map/ppermute | solution.py:300
  41.0 3.6 %collective-permute-done.2.swapped = bf16[3,64,4096]{2,1,0:T(8,128)(2,1)S(1)} collective-permute-done((bf16[3,64,4096]{2,1,0:T(8,128)(2,1)}, bf16[3,64,4096]{2,1,0:T(8,128)(2,1)S(1)}, u32[]{:S(2)}, u32[]{:S(2)}) %collective-permute-start.2) | collective-permute-done | bytes 1572896 | tf_op jit(solution)/shard_map/ppermute | solution.py:305
  44.6 1.9 %copy-done.4 = bf16[64,3,8192]{2,0,1:T(8,128)(2,1)S(1)} copy-done((bf16[64,3,8192]{2,0,1:T(8,128)(2,1)S(1)}, bf16[64,3,8192]{2,0,1:T(8,128)(2,1)}, u32[]{:S(2)}) %copy-start.4) | copy-done | bytes 3145752
  46.5 0.9 copy-done.9
  47.4 4.9 %dft_odd.1 = (bf16[3,16,4096]{2,1,0:T(8,128)(2,1)}, bf16[3,16,4096]{2,1,0:T(8,128)(2,1)}, bf16[3,16,4096]{2,1,0:T(8,128)(2,1)}, bf16[3,16,4096]{2,1,0:T(8,128)(2...) custom-call(s32[1]{0:T(128)} %bitcast.flags, ...), custom_call_target="tpu_custom_call" | custom-call | flops 30000001024 | bytes 30000001024 | tf_op jit(solution)/shard_map/dft_odd/pallas_call | solution.py:122
  53.8 7.3 %collective-permute-start.3 = (bf16[3,16,4096]{2,1,0:T(8,128)(2,1)}, bf16[3,16,4096]{2,1,0:T(8,128)(2,1)S(1)}, u32[]{:S(2)}, u32[]{:S(2)}) collective-permute-start(bf16[3,16,4096]{2,1,0:T(8,128)(2,1)} %get-tuple-element.27), channel_id=1, source_target_pairs={{0,8},{1,9},{2,10},{3,11},{4,12},{5,13},{6,14},{7,15},{8,0},{9,1},... | collective-permute-start | bytes 1179656 | tf_op jit(solution)/shard_map/ppermute | solution.py:286
  61.2 4.5 %collective-permute-start.5 = (bf16[3,16,4096]{2,1,0:T(8,128)(2,1)}, bf16[3,16,4096]{2,1,0:T(8,128)(2,1)S(1)}, u32[]{:S(2)}, u32[]{:S(2)}) collective-permute-start(bf16[3,16,4096]{2,1,0:T(8,128)(2,1)} %get-tuple-element.29), channel_id=1, source_target_pairs={{0,10},{1,11},{2,12},{3,13},{4,14},{5,15},{6,0},{7,1},{8,2},{9,3},... | collective-permute-start | bytes 1179656 | tf_op jit(solution)/shard_map/ppermute | solution.py:286
  66.6 2.7 %collective-permute-start.7 = (bf16[3,16,4096]{2,1,0:T(8,128)(2,1)}, bf16[3,16,4096]{2,1,0:T(8,128)(2,1)S(1)}, u32[]{:S(2)}, u32[]{:S(2)}) collective-permute-start(bf16[3,16,4096]{2,1,0:T(8,128)(2,1)} %get-tuple-element.31), channel_id=1, source_target_pairs={{0,12},{1,13},{2,14},{3,15},{4,0},{5,1},{6,2},{7,3},{8,4},{9,5},{1... | collective-permute-start | bytes 1179656 | tf_op jit(solution)/shard_map/ppermute | solution.py:286
  69.2 47.7 %all-to-all-done.evens = bf16[8,3,16,4096]{3,2,1,0:T(8,128)(2,1)} async-done(((bf16[8,3,16,4096]{3,2,1,0:T(8,128)(2,1)}), bf16[8,3,16,4096]{3,2,1,0:T(8,128)(2,1)}, u32[]{:S(2)}, u32[]{:S(2)}) %all-to-all-start) | async-done | bytes 3145760 | tf_op jit(solution)/shard_map/all_to_all | solution.py:304
  117.8 4.7 %held.1 = (bf16[8,3,16,4096]{3,2,1,0:T(8,128)(2,1)S(1)}, f32[3,8192]{1,0:T(4,128)S(1)}, bf16[16,256]{1,0:T(8,128)(2,1)S(1)}, bf16[512,128]{1,0:T(8,128)(2,1)S(1)}) custom-call(s32[1]{0:T(128)} %bitcast.flags, bf16[8,3,16,4096]{3,2,1,0:T(8,128)(2,1)} %all-to-all-done.evens, f32[3,8192]{1,0:T(4,128)S(1)} %copy-done.2), custom_call_target="tpu_custom_call" | custom-call | tf_op jit(solution)/shard_map/held/pallas_call | solution.py:173
  122.5 1.2 collective-permute-done.3.refs_1_
  123.8 5.8 %collective-permute-start.8 = (bf16[3,16,4096]{2,1,0:T(8,128)(2,1)S(1)}, bf16[3,16,4096]{2,1,0:T(8,128)(2,1)S(1)}, u32[]{:S(2)}, u32[]{:S(2)}) collective-permute-start(bf16[3,16,4096]{2,1,0:T(8,128)(2,1)S(1)} %copy-done.8), channel_id=1, source_target_pairs={{0,2},{1,3},{2,4},{3,5},{4,6},{5,7},{6,8},{7,9},{8,10},{9,11},{10,... | collective-permute-start | bytes 1179656 | tf_op jit(solution)/shard_map/ppermute | solution.py:286
  129.5 18.9 %collective-permute-done.4.refs_2_ = bf16[3,16,4096]{2,1,0:T(8,128)(2,1)S(1)} collective-permute-done((bf16[3,16,4096]{2,1,0:T(8,128)(2,1)}, bf16[3,16,4096]{2,1,0:T(8,128)(2,1)S(1)}, u32[]{:S(2)}, u32[]{:S(2)}) %collective-permute-start.4) | collective-permute-done | bytes 393248 | tf_op jit(solution)/shard_map/ppermute | solution.py:286
  148.5 13.2 %collective-permute-done.6.refs_4_ = bf16[3,16,4096]{2,1,0:T(8,128)(2,1)S(1)} collective-permute-done((bf16[3,16,4096]{2,1,0:T(8,128)(2,1)}, bf16[3,16,4096]{2,1,0:T(8,128)(2,1)S(1)}, u32[]{:S(2)}, u32[]{:S(2)}) %collective-permute-start.6) | collective-permute-done | bytes 393248 | tf_op jit(solution)/shard_map/ppermute | solution.py:286
  161.6 3.3 %collective-permute-done.8.refs_6_ = bf16[3,16,4096]{2,1,0:T(8,128)(2,1)S(1)} collective-permute-done((bf16[3,16,4096]{2,1,0:T(8,128)(2,1)S(1)}, bf16[3,16,4096]{2,1,0:T(8,128)(2,1)S(1)}, u32[]{:S(2)}, u32[]{:S(2)}) %collective-permute-start.8) | collective-permute-done | bytes 393248 | tf_op jit(solution)/shard_map/ppermute | solution.py:286
  164.9 2.5 %gram.1 = f32[16,16,128]{2,1,0:T(8,128)S(1)} custom-call(bf16[16,256]{1,0:T(8,128)(2,1)S(1)} %get-tuple-element.20.left, bf16[512,128]{1,0:T(8,128)(2,1)S(1)} %get-tuple-element.21.right, f32[3,8192]{1,0:T(4,128)S(1)} %get-tuple-element.25.weights, bf16[8,3,16,4096]{3,2,1,0:T(8,128)(2,1)S(1)} %get-tuple-element.26.refs_0_, ...), custom_call_target="tpu_custom_call" | custom-call | tf_op jit(solution)/shard_map/gram/pallas_call | solution.py:214
  167.4 13.3 %all_to_all.10.grams = f32[16,16,128]{2,1,0:T(8,128)S(1)} all-to-all(f32[16,16,128]{2,1,0:T(8,128)S(1)} %gram.1), channel_id=1, replica_groups=mesh['pts'=16,'tm'=16] {'pts'}, dimensions={0} | all-to-all | bytes 262144 | tf_op jit(solution)/shard_map/all_to_all | solution.py:313
  180.7 4.0 %modes.1 = bf16[4,16,3,2,8192]{4,3,2,1,0:T(2,128)(2,1)} custom-call(s32[1]{0:T(128)} %bitcast.flags, f32[16,16,128]{2,1,0:T(8,128)S(1)} %all_to_all.10.grams, bf16[8,3,16,4096]{3,2,1,0:T(8,128)(2,1)S(1)} %get-tuple-element.26.refs_0_, bf16[3,16,4096]{2,1,0:T(8,128)(2,1)S(1)} %collective-permute-done.3.refs_1_, ...), custom_call_target="tpu_custom_call" | custom-call | tf_op jit(solution)/shard_map/modes/pallas_call | solution.py:270
  (25 shorter events, 4.8 us)
Async XLA Ops:
  0.0 8.9 %copy-start = (bf16[64,3,8192]{2,0,1:T(8,128)(2,1)S(1)}, bf16[64,3,8192]{2,0,1:T(8,128)(2,1)}, u32[]{:S(2)}) copy-start(bf16[64,3,8192]{2,0,1:T(8,128)(2,1)} %param.5) | copy-start | bytes 9437188
  0.0 8.9 %collective-permute-start = (bf16[3,64,8192]{2,1,0:T(8,128)(2,1)}, bf16[3,64,8192]{2,1,0:T(8,128)(2,1)}, u32[]{:S(2)}, u32[]{:S(2)}) collective-permute-start(bf16[3,64,8192]{2,1,0:T(8,128)(2,1)} %bitcast.6), channel_id=1, source_target_pairs={{0,1},{1,0},{2,3},{3,2},{4,5},{5,4},{6,7},{7,6},{8,9},{9,8},{10,11... | collective-permute-start | bytes 9437192 | tf_op jit(solution)/shard_map/ppermute | solution.py:301
  6.0 34.9 %collective-permute-start.1 = (bf16[3,64,4096]{2,1,0:T(8,128)(2,1)}, bf16[3,64,4096]{2,1,0:T(8,128)(2,1)}, u32[]{:S(2)}, u32[]{:S(2)}) collective-permute-start(bf16[3,64,4096]{2,1,0:T(8,128)(2,1)} %dynamic-slice_bitcast_fusion), channel_id=1, source_target_pairs={{2,0},{4,2},{6,4},{8,6},{10,8},{12,10},{14,12},{15,1},{1,3},{3,5},... | collective-permute-start | bytes 4718600 | tf_op jit(solution)/shard_map/ppermute | solution.py:300
  8.9 0.8 copy-start.3
  13.2 1.7 copy-start.1
  14.9 102.1 %all-to-all-start = ((bf16[8,3,16,4096]{3,2,1,0:T(8,128)(2,1)}), bf16[8,3,16,4096]{3,2,1,0:T(8,128)(2,1)}, u32[]{:S(2)}, u32[]{:S(2)}) async-start(bf16[8,3,16,4096]{3,2,1,0:T(8,128)(2,1)} %copy-done.1), calls=%async_computation | async-start | bytes 6291456 | tf_op jit(solution)/shard_map/all_to_all | solution.py:304
  41.0 3.6 %collective-permute-start.2 = (bf16[3,64,4096]{2,1,0:T(8,128)(2,1)}, bf16[3,64,4096]{2,1,0:T(8,128)(2,1)S(1)}, u32[]{:S(2)}, u32[]{:S(2)}) collective-permute-start(bf16[3,64,4096]{2,1,0:T(8,128)(2,1)} %collective-permute-done.1.halo), channel_id=1, source_target_pairs={{0,1},{1,0},{2,3},{3,2},{4,5},{5,4},{6,7},{7,6},{8,9},{9,8},{10,11... | collective-permute-start | bytes 4718600 | tf_op jit(solution)/shard_map/ppermute | solution.py:305
  44.6 1.9 %copy-start.4 = (bf16[64,3,8192]{2,0,1:T(8,128)(2,1)S(1)}, bf16[64,3,8192]{2,0,1:T(8,128)(2,1)}, u32[]{:S(2)}) copy-start(bf16[64,3,8192]{2,0,1:T(8,128)(2,1)} %param.6) | copy-start | bytes 9437188
  46.5 0.9 copy-start.9
  52.4 0.7 copy-start.5
  53.1 0.7 copy-start.7
  53.8 69.9 %collective-permute-start.3 = (bf16[3,16,4096]{2,1,0:T(8,128)(2,1)}, bf16[3,16,4096]{2,1,0:T(8,128)(2,1)S(1)}, u32[]{:S(2)}, u32[]{:S(2)}) collective-permute-start(bf16[3,16,4096]{2,1,0:T(8,128)(2,1)} %get-tuple-element.27), channel_id=1, source_target_pairs={{0,8},{1,9},{2,10},{3,11},{4,12},{5,13},{6,14},{7,15},{8,0},{9,1},... | collective-permute-start | bytes 1179656 | tf_op jit(solution)/shard_map/ppermute | solution.py:286
  61.2 87.3 %collective-permute-start.4 = (bf16[3,16,4096]{2,1,0:T(8,128)(2,1)}, bf16[3,16,4096]{2,1,0:T(8,128)(2,1)S(1)}, u32[]{:S(2)}, u32[]{:S(2)}) collective-permute-start(bf16[3,16,4096]{2,1,0:T(8,128)(2,1)} %get-tuple-element.28), channel_id=1, source_target_pairs={{0,6},{1,7},{2,8},{3,9},{4,10},{5,11},{6,12},{7,13},{8,14},{9,15},... | collective-permute-start | bytes 1179656 | tf_op jit(solution)/shard_map/ppermute | solution.py:286
  61.2 87.3 %collective-permute-start.5 = (bf16[3,16,4096]{2,1,0:T(8,128)(2,1)}, bf16[3,16,4096]{2,1,0:T(8,128)(2,1)S(1)}, u32[]{:S(2)}, u32[]{:S(2)}) collective-permute-start(bf16[3,16,4096]{2,1,0:T(8,128)(2,1)} %get-tuple-element.29), channel_id=1, source_target_pairs={{0,10},{1,11},{2,12},{3,13},{4,14},{5,15},{6,0},{7,1},{8,2},{9,3},... | collective-permute-start | bytes 1179656 | tf_op jit(solution)/shard_map/ppermute | solution.py:286
  65.7 96.0 %collective-permute-start.6 = (bf16[3,16,4096]{2,1,0:T(8,128)(2,1)}, bf16[3,16,4096]{2,1,0:T(8,128)(2,1)S(1)}, u32[]{:S(2)}, u32[]{:S(2)}) collective-permute-start(bf16[3,16,4096]{2,1,0:T(8,128)(2,1)} %get-tuple-element.30), channel_id=1, source_target_pairs={{0,4},{1,5},{2,6},{3,7},{4,8},{5,9},{6,10},{7,11},{8,12},{9,13},{1... | collective-permute-start | bytes 1179656 | tf_op jit(solution)/shard_map/ppermute | solution.py:286
  66.6 95.1 %collective-permute-start.7 = (bf16[3,16,4096]{2,1,0:T(8,128)(2,1)}, bf16[3,16,4096]{2,1,0:T(8,128)(2,1)S(1)}, u32[]{:S(2)}, u32[]{:S(2)}) collective-permute-start(bf16[3,16,4096]{2,1,0:T(8,128)(2,1)} %get-tuple-element.31), channel_id=1, source_target_pairs={{0,12},{1,13},{2,14},{3,15},{4,0},{5,1},{6,2},{7,3},{8,4},{9,5},{1... | collective-permute-start | bytes 1179656 | tf_op jit(solution)/shard_map/ppermute | solution.py:286
  116.9 0.9 copy-start.2
  117.8 5.9 %copy-start.8 = (bf16[3,16,4096]{2,1,0:T(8,128)(2,1)S(1)}, bf16[3,16,4096]{2,1,0:T(8,128)(2,1)}, u32[]{:S(2)}) copy-start(bf16[3,16,4096]{2,1,0:T(8,128)(2,1)} %copy-done.7) | copy-start | bytes 1179652
  117.8 30.6 %copy-start.6 = (bf16[3,16,4096]{2,1,0:T(8,128)(2,1)S(1)}, bf16[3,16,4096]{2,1,0:T(8,128)(2,1)}, u32[]{:S(2)}) copy-start(bf16[3,16,4096]{2,1,0:T(8,128)(2,1)} %copy-done.5) | copy-start | bytes 1179652
  123.8 41.1 %collective-permute-start.8 = (bf16[3,16,4096]{2,1,0:T(8,128)(2,1)S(1)}, bf16[3,16,4096]{2,1,0:T(8,128)(2,1)S(1)}, u32[]{:S(2)}, u32[]{:S(2)}) collective-permute-start(bf16[3,16,4096]{2,1,0:T(8,128)(2,1)S(1)} %copy-done.8), channel_id=1, source_target_pairs={{0,2},{1,3},{2,4},{3,5},{4,6},{5,7},{6,8},{7,9},{8,10},{9,11},{10,... | collective-permute-start | bytes 1179656 | tf_op jit(solution)/shard_map/ppermute | solution.py:286
  148.5 16.4 %collective-permute-start.9 = (bf16[3,16,4096]{2,1,0:T(8,128)(2,1)S(1)}, bf16[3,16,4096]{2,1,0:T(8,128)(2,1)S(1)}, u32[]{:S(2)}, u32[]{:S(2)}) collective-permute-start(bf16[3,16,4096]{2,1,0:T(8,128)(2,1)S(1)} %copy-done.6), channel_id=1, source_target_pairs={{0,14},{1,15},{2,0},{3,1},{4,2},{5,3},{6,4},{7,5},{8,6},{9,7},{10,... | collective-permute-start | bytes 1179656 | tf_op jit(solution)/shard_map/ppermute | solution.py:286

commit v6 on v4

--- a/solution.py
+++ b/solution.py
@@ -24,7 +24,7 @@
 HELD = 6
 WIDE = 4096
 VMEM_LIMIT = 28 * 1024 * 1024
-SHIFTS = (4, 3, 5, 2, 6, 1, 7, 0)
+SHIFTS = (2, 6, 3, 5, 4, 1, 7, 0)
 
 
 def window_tables():

time: 185 us -> 186 us (level)
  waiting for transfers between devices: 109 us -> 111 us
  starting transfers between devices: 32.8 us -> 30.8 us
    ppermute x7, waiting for transfers between devices: 37 us -> 50.4 us  [shifted_by(): return lax.ppermute(value, 'tm', pairs)]
    all_to_all x1, waiting for transfers between devices: 47.7 us -> 36.3 us  [shards(): lax.all_to_all(evens, 'tm', split_axis=0, concat_axis=0, axis_index_group...]
    ppermute x7, starting transfers between devices: 21 us -> 18.9 us  [shifted_by(): return lax.ppermute(value, 'tm', pairs)]
  transfers between devices with their start and end apart: 11 -> 11, of which waited for: 8 -> 7; matrix products, arithmetic and copies ran while one was open for 2% -> 2% of each run, Pallas kernels for 7% -> 7%
where the time goes in v6:
time: 186 us; the launch traced here: 185 us
  waiting for transfers between devices  111 us (60%)
  starting transfers between devices  30.8 us (17%)
  Pallas kernels  19.6 us (11%)
  blocking collectives  13.7 us (7%)
  local copies, waits for them, and re-layouts  10.4 us (6%)
    ppermute x7, waiting for transfers between devices, shifted_by(): return lax.ppermute(value, 'tm', pairs)  50.4 us
    all_to_all x1, waiting for transfers between devices, shards(): lax.all_to_all(evens, 'tm', split_axis=0, concat_axis=0, axis_index_group...  36.3 us
    ppermute x1, waiting for transfers between devices, shards(): halo = lax.ppermute(own, 'tm', before + after)  19.5 us
    ppermute x7, starting transfers between devices, shifted_by(): return lax.ppermute(value, 'tm', pairs)  18.9 us
    all_to_all x1, blocking collectives, shards(): lax.all_to_all(grams, 'pts', split_axis=0, concat_axis=0, tiled=True)  13.7 us
    unnamed x20, local copies, waits for them, and re-layouts  7.65 us
    all_to_all x1, starting transfers between devices, shards(): lax.all_to_all(evens, 'tm', split_axis=0, concat_axis=0, axis_index_group...  6.56 us
    pallas_call x1, Pallas kernels, dft_odd(): pl.pallas_call(dft_odd_kernel, grid_spec=pltpu.PrefetchScalarGridSpec(num...  4.94 us
  transfers between devices with their start and end apart: 11, of which 7 were waited for; matrix products, arithmetic and copies ran while one was open for 2% of the time, Pallas kernels for 7%

profile of v6, /device:TPU:1, one launch (start us, length us, event | category | flops | bytes accessed | tf_op | source)
XLA Modules:
  0.0 185.2 jit_solution(10814578229834536936)
XLA Ops:
  0.0 3.2 %collective-permute-start = (bf16[3,64,8192]{2,1,0:T(8,128)(2,1)}, bf16[3,64,8192]{2,1,0:T(8,128)(2,1)}, u32[]{:S(2)}, u32[]{:S(2)}) collective-permute-start(bf16[3,64,8192]{2,1,0:T(8,128)(2,1)} %bitcast.6), channel_id=1, source_target_pairs={{0,1},{1,0},{2,3},{3,2},{4,5},{5,4},{6,7},{7,6},{8,9},{9,8},{10,11... | collective-permute-start | bytes 9437192 | tf_op jit(solution)/shard_map/ppermute | solution.py:295
  3.2 2.8 %dynamic-slice_bitcast_fusion = bf16[3,64,4096]{2,1,0:T(8,128)(2,1)} fusion(bf16[64,3,8192]{2,0,1:T(8,128)(2,1)} %param.5, s32[]{:T(128)S(6)} %select_n.3), kind=kLoop, calls=%fused_computation | loop fusion | bytes 3145732 | tf_op jit(solution)/shard_map/dynamic_slice | solution.py:291
  6.0 2.1 %collective-permute-start.1 = (bf16[3,64,4096]{2,1,0:T(8,128)(2,1)}, bf16[3,64,4096]{2,1,0:T(8,128)(2,1)}, u32[]{:S(2)}, u32[]{:S(2)}) collective-permute-start(bf16[3,64,4096]{2,1,0:T(8,128)(2,1)} %dynamic-slice_bitcast_fusion), channel_id=1, source_target_pairs={{2,0},{4,2},{6,4},{8,6},{10,8},{12,10},{14,12},{15,1},{1,3},{3,5},... | collective-permute-start | bytes 4718600 | tf_op jit(solution)/shard_map/ppermute | solution.py:294
  9.6 3.6 %dft_even.1 = bf16[8,3,16,4096]{3,2,1,0:T(8,128)(2,1)S(1)} custom-call(s32[1]{0:T(128)} %bitcast.flags, bf16[2,64,128]{2,1,0:T(8,128)(2,1)S(1)} %copy-done.3, bf16[3,64,8192]{2,1,0:T(8,128)(2,1)S(1)} %bitcast.7, bf16[3,64,8192]{2,1,0:T(8,128)(2,1)S(1)} %bitcast.8, bf16[3,64,8192]{2,1,0:T(8,128)(2,1)} %collective-permute-done.beside_a.beside_b, ...), custom_call_target="tpu_custom_call" | custom-call | tf_op jit(solution)/shard_map/dft_even/pallas_call | solution.py:75
  13.2 1.7 copy-done.1
  14.9 6.6 %all-to-all-start = ((bf16[8,3,16,4096]{3,2,1,0:T(8,128)(2,1)}), bf16[8,3,16,4096]{3,2,1,0:T(8,128)(2,1)}, u32[]{:S(2)}, u32[]{:S(2)}) async-start(bf16[8,3,16,4096]{3,2,1,0:T(8,128)(2,1)} %copy-done.1), calls=%async_computation | async-start | bytes 6291456 | tf_op jit(solution)/shard_map/all_to_all | solution.py:298
  21.4 19.5 %collective-permute-done.1.halo = bf16[3,64,4096]{2,1,0:T(8,128)(2,1)} collective-permute-done((bf16[3,64,4096]{2,1,0:T(8,128)(2,1)}, bf16[3,64,4096]{2,1,0:T(8,128)(2,1)}, u32[]{:S(2)}, u32[]{:S(2)}) %collective-permute-start.1) | collective-permute-done | bytes 1572896 | tf_op jit(solution)/shard_map/ppermute | solution.py:294
  41.0 3.6 %collective-permute-done.2.swapped = bf16[3,64,4096]{2,1,0:T(8,128)(2,1)S(1)} collective-permute-done((bf16[3,64,4096]{2,1,0:T(8,128)(2,1)}, bf16[3,64,4096]{2,1,0:T(8,128)(2,1)S(1)}, u32[]{:S(2)}, u32[]{:S(2)}) %collective-permute-start.2) | collective-permute-done | bytes 1572896 | tf_op jit(solution)/shard_map/ppermute | solution.py:299
  44.6 1.9 %copy-done.4 = bf16[64,3,8192]{2,0,1:T(8,128)(2,1)S(1)} copy-done((bf16[64,3,8192]{2,0,1:T(8,128)(2,1)S(1)}, bf16[64,3,8192]{2,0,1:T(8,128)(2,1)}, u32[]{:S(2)}) %copy-start.4) | copy-done | bytes 3145752
  46.5 0.9 copy-done.9
  47.4 4.9 %dft_odd.1 = (bf16[3,16,4096]{2,1,0:T(8,128)(2,1)}, bf16[3,16,4096]{2,1,0:T(8,128)(2,1)}, bf16[3,16,4096]{2,1,0:T(8,128)(2,1)}, bf16[3,16,4096]{2,1,0:T(8,128)(2...) custom-call(s32[1]{0:T(128)} %bitcast.flags, ...), custom_call_target="tpu_custom_call" | custom-call | flops 30000001024 | bytes 30000001024 | tf_op jit(solution)/shard_map/dft_odd/pallas_call | solution.py:122
  54.6 5.4 %collective-permute-start.4 = (bf16[3,16,4096]{2,1,0:T(8,128)(2,1)}, bf16[3,16,4096]{2,1,0:T(8,128)(2,1)S(1)}, u32[]{:S(2)}, u32[]{:S(2)}) collective-permute-start(bf16[3,16,4096]{2,1,0:T(8,128)(2,1)} %get-tuple-element.24), channel_id=1, source_target_pairs={{0,12},{1,13},{2,14},{3,15},{4,0},{5,1},{6,2},{7,3},{8,4},{9,5},{1... | collective-permute-start | bytes 1179656 | tf_op jit(solution)/shard_map/ppermute | solution.py:280
  60.0 4.5 %collective-permute-start.6 = (bf16[3,16,4096]{2,1,0:T(8,128)(2,1)}, bf16[3,16,4096]{2,1,0:T(8,128)(2,1)S(1)}, u32[]{:S(2)}, u32[]{:S(2)}) collective-permute-start(bf16[3,16,4096]{2,1,0:T(8,128)(2,1)} %get-tuple-element.26), channel_id=1, source_target_pairs={{0,10},{1,11},{2,12},{3,13},{4,14},{5,15},{6,0},{7,1},{8,2},{9,3},... | collective-permute-start | bytes 1179656 | tf_op jit(solution)/shard_map/ppermute | solution.py:280
  64.5 4.7 %collective-permute-start.7 = (bf16[3,16,4096]{2,1,0:T(8,128)(2,1)}, bf16[3,16,4096]{2,1,0:T(8,128)(2,1)S(1)}, u32[]{:S(2)}, u32[]{:S(2)}) collective-permute-start(bf16[3,16,4096]{2,1,0:T(8,128)(2,1)} %get-tuple-element.27), channel_id=1, source_target_pairs={{0,8},{1,9},{2,10},{3,11},{4,12},{5,13},{6,14},{7,15},{8,0},{9,1},... | collective-permute-start | bytes 1179656 | tf_op jit(solution)/shard_map/ppermute | solution.py:280
  69.2 36.3 %all-to-all-done.evens = bf16[8,3,16,4096]{3,2,1,0:T(8,128)(2,1)} async-done(((bf16[8,3,16,4096]{3,2,1,0:T(8,128)(2,1)}), bf16[8,3,16,4096]{3,2,1,0:T(8,128)(2,1)}, u32[]{:S(2)}, u32[]{:S(2)}) %all-to-all-start) | async-done | bytes 3145760 | tf_op jit(solution)/shard_map/all_to_all | solution.py:298
  105.6 0.9 copy-done.2
  106.5 4.4 %held.1 = (bf16[8,3,16,4096]{3,2,1,0:T(8,128)(2,1)S(1)}, f32[3,8192]{1,0:T(4,128)S(1)}) custom-call(bf16[8,3,16,4096]{3,2,1,0:T(8,128)(2,1)} %all-to-all-done.evens, f32[3,8192]{1,0:T(4,128)S(1)} %copy-done.2), custom_call_target="tpu_custom_call" | custom-call | tf_op jit(solution)/shard_map/held/pallas_call | solution.py:162
  110.9 14.5 %collective-permute-done.3.refs_1_ = bf16[3,16,4096]{2,1,0:T(8,128)(2,1)S(1)} collective-permute-done((bf16[3,16,4096]{2,1,0:T(8,128)(2,1)}, bf16[3,16,4096]{2,1,0:T(8,128)(2,1)S(1)}, u32[]{:S(2)}, u32[]{:S(2)}) %collective-permute-start.3) | collective-permute-done | bytes 393248 | tf_op jit(solution)/shard_map/ppermute | solution.py:280
  126.1 2.9 %collective-permute-start.9 = (bf16[3,16,4096]{2,1,0:T(8,128)(2,1)S(1)}, bf16[3,16,4096]{2,1,0:T(8,128)(2,1)S(1)}, u32[]{:S(2)}, u32[]{:S(2)}) collective-permute-start(bf16[3,16,4096]{2,1,0:T(8,128)(2,1)S(1)} %copy-done.6), channel_id=1, source_target_pairs={{0,14},{1,15},{2,0},{3,1},{4,2},{5,3},{6,4},{7,5},{8,6},{9,7},{10,... | collective-permute-start | bytes 1179656 | tf_op jit(solution)/shard_map/ppermute | solution.py:280
  129.0 29.9 %collective-permute-done.5.refs_3_ = bf16[3,16,4096]{2,1,0:T(8,128)(2,1)S(1)} collective-permute-done((bf16[3,16,4096]{2,1,0:T(8,128)(2,1)}, bf16[3,16,4096]{2,1,0:T(8,128)(2,1)S(1)}, u32[]{:S(2)}, u32[]{:S(2)}) %collective-permute-start.5) | collective-permute-done | bytes 393248 | tf_op jit(solution)/shard_map/ppermute | solution.py:280
  158.9 6.0 %collective-permute-done.8.refs_6_ = bf16[3,16,4096]{2,1,0:T(8,128)(2,1)S(1)} collective-permute-done((bf16[3,16,4096]{2,1,0:T(8,128)(2,1)S(1)}, bf16[3,16,4096]{2,1,0:T(8,128)(2,1)S(1)}, u32[]{:S(2)}, u32[]{:S(2)}) %collective-permute-start.8) | collective-permute-done | bytes 393248 | tf_op jit(solution)/shard_map/ppermute | solution.py:280
  164.9 2.6 %gram.1 = f32[16,16,128]{2,1,0:T(8,128)S(1)} custom-call(s32[1]{0:T(128)} %bitcast.flags, f32[3,8192]{1,0:T(4,128)S(1)} %get-tuple-element.21.weights, bf16[8,3,16,4096]{3,2,1,0:T(8,128)(2,1)S(1)} %get-tuple-element.22.refs_0_, bf16[3,16,4096]{2,1,0:T(8,128)(2,1)S(1)} %collective-permute-done.3.refs_1_, ...), custom_call_target="tpu_custom_call" | custom-call | tf_op jit(solution)/shard_map/gram/pallas_call | solution.py:208
  167.5 13.7 %all_to_all.10.grams = f32[16,16,128]{2,1,0:T(8,128)S(1)} all-to-all(f32[16,16,128]{2,1,0:T(8,128)S(1)} %gram.1), channel_id=1, replica_groups=mesh['pts'=16,'tm'=16] {'pts'}, dimensions={0} | all-to-all | bytes 262144 | tf_op jit(solution)/shard_map/all_to_all | solution.py:307
  181.2 4.0 %modes.1 = bf16[4,16,3,2,8192]{4,3,2,1,0:T(2,128)(2,1)} custom-call(s32[1]{0:T(128)} %bitcast.flags, f32[16,16,128]{2,1,0:T(8,128)S(1)} %all_to_all.10.grams, bf16[8,3,16,4096]{3,2,1,0:T(8,128)(2,1)S(1)} %get-tuple-element.22.refs_0_, bf16[3,16,4096]{2,1,0:T(8,128)(2,1)S(1)} %collective-permute-done.3.refs_1_, ...), custom_call_target="tpu_custom_call" | custom-call | tf_op jit(solution)/shard_map/modes/pallas_call | solution.py:264
  (25 shorter events, 4.4 us)
Async XLA Ops:
  0.0 8.9 %copy-start = (bf16[64,3,8192]{2,0,1:T(8,128)(2,1)S(1)}, bf16[64,3,8192]{2,0,1:T(8,128)(2,1)}, u32[]{:S(2)}) copy-start(bf16[64,3,8192]{2,0,1:T(8,128)(2,1)} %param.5) | copy-start | bytes 9437188
  0.0 8.9 %collective-permute-start = (bf16[3,64,8192]{2,1,0:T(8,128)(2,1)}, bf16[3,64,8192]{2,1,0:T(8,128)(2,1)}, u32[]{:S(2)}, u32[]{:S(2)}) collective-permute-start(bf16[3,64,8192]{2,1,0:T(8,128)(2,1)} %bitcast.6), channel_id=1, source_target_pairs={{0,1},{1,0},{2,3},{3,2},{4,5},{5,4},{6,7},{7,6},{8,9},{9,8},{10,11... | collective-permute-start | bytes 9437192 | tf_op jit(solution)/shard_map/ppermute | solution.py:295
  6.0 34.9 %collective-permute-start.1 = (bf16[3,64,4096]{2,1,0:T(8,128)(2,1)}, bf16[3,64,4096]{2,1,0:T(8,128)(2,1)}, u32[]{:S(2)}, u32[]{:S(2)}) collective-permute-start(bf16[3,64,4096]{2,1,0:T(8,128)(2,1)} %dynamic-slice_bitcast_fusion), channel_id=1, source_target_pairs={{2,0},{4,2},{6,4},{8,6},{10,8},{12,10},{14,12},{15,1},{1,3},{3,5},... | collective-permute-start | bytes 4718600 | tf_op jit(solution)/shard_map/ppermute | solution.py:294
  8.9 0.8 copy-start.3
  13.2 1.7 copy-start.1
  14.9 90.7 %all-to-all-start = ((bf16[8,3,16,4096]{3,2,1,0:T(8,128)(2,1)}), bf16[8,3,16,4096]{3,2,1,0:T(8,128)(2,1)}, u32[]{:S(2)}, u32[]{:S(2)}) async-start(bf16[8,3,16,4096]{3,2,1,0:T(8,128)(2,1)} %copy-done.1), calls=%async_computation | async-start | bytes 6291456 | tf_op jit(solution)/shard_map/all_to_all | solution.py:298
  41.0 3.6 %collective-permute-start.2 = (bf16[3,64,4096]{2,1,0:T(8,128)(2,1)}, bf16[3,64,4096]{2,1,0:T(8,128)(2,1)S(1)}, u32[]{:S(2)}, u32[]{:S(2)}) collective-permute-start(bf16[3,64,4096]{2,1,0:T(8,128)(2,1)} %collective-permute-done.1.halo), channel_id=1, source_target_pairs={{0,1},{1,0},{2,3},{3,2},{4,5},{5,4},{6,7},{7,6},{8,9},{9,8},{10,11... | collective-permute-start | bytes 4718600 | tf_op jit(solution)/shard_map/ppermute | solution.py:299
  44.6 1.9 %copy-start.4 = (bf16[64,3,8192]{2,0,1:T(8,128)(2,1)S(1)}, bf16[64,3,8192]{2,0,1:T(8,128)(2,1)}, u32[]{:S(2)}) copy-start(bf16[64,3,8192]{2,0,1:T(8,128)(2,1)} %param.6) | copy-start | bytes 9437188
  46.5 0.9 copy-start.9
  52.4 0.7 copy-start.5
  53.1 0.7 copy-start.7
  53.8 71.6 %collective-permute-start.3 = (bf16[3,16,4096]{2,1,0:T(8,128)(2,1)}, bf16[3,16,4096]{2,1,0:T(8,128)(2,1)S(1)}, u32[]{:S(2)}, u32[]{:S(2)}) collective-permute-start(bf16[3,16,4096]{2,1,0:T(8,128)(2,1)} %get-tuple-element.23), channel_id=1, source_target_pairs={{0,4},{1,5},{2,6},{3,7},{4,8},{5,9},{6,10},{7,11},{8,12},{9,13},{1... | collective-permute-start | bytes 1179656 | tf_op jit(solution)/shard_map/ppermute | solution.py:280
  54.6 71.4 %collective-permute-start.4 = (bf16[3,16,4096]{2,1,0:T(8,128)(2,1)}, bf16[3,16,4096]{2,1,0:T(8,128)(2,1)S(1)}, u32[]{:S(2)}, u32[]{:S(2)}) collective-permute-start(bf16[3,16,4096]{2,1,0:T(8,128)(2,1)} %get-tuple-element.24), channel_id=1, source_target_pairs={{0,12},{1,13},{2,14},{3,15},{4,0},{5,1},{6,2},{7,3},{8,4},{9,5},{1... | collective-permute-start | bytes 1179656 | tf_op jit(solution)/shard_map/ppermute | solution.py:280
  60.0 98.9 %collective-permute-start.5 = (bf16[3,16,4096]{2,1,0:T(8,128)(2,1)}, bf16[3,16,4096]{2,1,0:T(8,128)(2,1)S(1)}, u32[]{:S(2)}, u32[]{:S(2)}) collective-permute-start(bf16[3,16,4096]{2,1,0:T(8,128)(2,1)} %get-tuple-element.25), channel_id=1, source_target_pairs={{0,6},{1,7},{2,8},{3,9},{4,10},{5,11},{6,12},{7,13},{8,14},{9,15},... | collective-permute-start | bytes 1179656 | tf_op jit(solution)/shard_map/ppermute | solution.py:280
  60.0 98.9 %collective-permute-start.6 = (bf16[3,16,4096]{2,1,0:T(8,128)(2,1)}, bf16[3,16,4096]{2,1,0:T(8,128)(2,1)S(1)}, u32[]{:S(2)}, u32[]{:S(2)}) collective-permute-start(bf16[3,16,4096]{2,1,0:T(8,128)(2,1)} %get-tuple-element.26), channel_id=1, source_target_pairs={{0,10},{1,11},{2,12},{3,13},{4,14},{5,15},{6,0},{7,1},{8,2},{9,3},... | collective-permute-start | bytes 1179656 | tf_op jit(solution)/shard_map/ppermute | solution.py:280
  64.5 94.4 %collective-permute-start.7 = (bf16[3,16,4096]{2,1,0:T(8,128)(2,1)}, bf16[3,16,4096]{2,1,0:T(8,128)(2,1)S(1)}, u32[]{:S(2)}, u32[]{:S(2)}) collective-permute-start(bf16[3,16,4096]{2,1,0:T(8,128)(2,1)} %get-tuple-element.27), channel_id=1, source_target_pairs={{0,8},{1,9},{2,10},{3,11},{4,12},{5,13},{6,14},{7,15},{8,0},{9,1},... | collective-permute-start | bytes 1179656 | tf_op jit(solution)/shard_map/ppermute | solution.py:280
  105.6 0.9 copy-start.2
  106.5 19.0 %copy-start.8 = (bf16[3,16,4096]{2,1,0:T(8,128)(2,1)S(1)}, bf16[3,16,4096]{2,1,0:T(8,128)(2,1)}, u32[]{:S(2)}) copy-start(bf16[3,16,4096]{2,1,0:T(8,128)(2,1)} %copy-done.7) | copy-start | bytes 1179652
  106.5 19.6 %copy-start.6 = (bf16[3,16,4096]{2,1,0:T(8,128)(2,1)S(1)}, bf16[3,16,4096]{2,1,0:T(8,128)(2,1)}, u32[]{:S(2)}) copy-start(bf16[3,16,4096]{2,1,0:T(8,128)(2,1)} %copy-done.5) | copy-start | bytes 1179652
  125.5 39.4 %collective-permute-start.8 = (bf16[3,16,4096]{2,1,0:T(8,128)(2,1)S(1)}, bf16[3,16,4096]{2,1,0:T(8,128)(2,1)S(1)}, u32[]{:S(2)}, u32[]{:S(2)}) collective-permute-start(bf16[3,16,4096]{2,1,0:T(8,128)(2,1)S(1)} %copy-done.8), channel_id=1, source_target_pairs={{0,2},{1,3},{2,4},{3,5},{4,6},{5,7},{6,8},{7,9},{8,10},{9,11},{10,... | collective-permute-start | bytes 1179656 | tf_op jit(solution)/shard_map/ppermute | solution.py:280
  126.1 38.8 %collective-permute-start.9 = (bf16[3,16,4096]{2,1,0:T(8,128)(2,1)S(1)}, bf16[3,16,4096]{2,1,0:T(8,128)(2,1)S(1)}, u32[]{:S(2)}, u32[]{:S(2)}) collective-permute-start(bf16[3,16,4096]{2,1,0:T(8,128)(2,1)S(1)} %copy-done.6), channel_id=1, source_target_pairs={{0,14},{1,15},{2,0},{3,1},{4,2},{5,3},{6,4},{7,5},{8,6},{9,7},{10,... | collective-permute-start | bytes 1179656 | tf_op jit(solution)/shard_map/ppermute | solution.py:280
